TPU v7x, 32 devices: a whole 2x2x4 slice. The times are simulated.
32 devices in a mesh: ctx: 16 (over z, y, x), head: 2 (over core).
Axes of the slice: x: 2, y: 2, z: 4, core: 2. Of those that a mesh axis runs over, the one named last changes fastest.
Arguments:
- queries: bfloat16 [2048, 4096], P('ctx', 'head'), may hold values from -45 to 45
- kv_rows: bfloat16 [2048, 512], P('ctx'), may hold values from -6 to 6
- doc_start: int32 [64], replicated, may hold values from 0 to 2016, as said below
- destination: int32 [64], replicated, may hold values from 0 to 63, as said below
- out_weight: bfloat16 [4096, 2048], P('head'), may hold values from -0.5 to 0.5
Outputs:
- mixed: bfloat16 [2048, 2048], P('head', 'ctx')
Inputs may be any that keep to these rules, and one draw needn't show every extreme that they name: Documents are runs of whole blocks: doc_start[b] is a multiple of 32, at most b * 32, never falls from block to block, and equals b * 32 where a document begins; doc_start[0] = 0. `destination`: A permutation of 0 .. 63 that maps every aligned group of 16 consecutive blocks onto itself.
All inputs are finite; a program needn't handle non-finite values.
Results may differ from a plain program's by a relative error of at most 0.011.
Values may be sent and summed in bfloat16 or wider, within the bound.
No kernel may reach another device: no remote copies, remote signals or barrier semaphores. Data moves between devices by JAX's collectives and lax.ppermute only.
A program may use at most 64 MiB of HBM per device.

v0:
```python
import functools
import jax, jax.numpy as jnp, numpy as np
from jax import lax
from jax.experimental import pallas as pl
from jax.experimental.pallas import tpu as pltpu
from jax.sharding import PartitionSpec as P

DH=128; W1=512; W2=32; QB=32
HG=4
ROWS=W1+QB
VR=DH+16
CH=2
NCH=W2//CH
LOG2E=1.4426950408889634

def att_kernel(inval_ref, q_ref, kv_ref, e_ref, out_ref, k1x, v1t, v2e, k2f, qs, sbuf, acc):
    b=pl.program_id(0); g=pl.program_id(1)
    lanes=HG*QB
    @pl.when(g==0)
    def _():
        inv=inval_ref[b]
        start=pl.multiple_of(b*QB,QB)
        k1=kv_ref[pl.ds(start,ROWS),0:DH].astype(jnp.float32)
        row=lax.broadcasted_iota(jnp.int32,(ROWS,DH),0)
        ok=row>=inv
        k1x[...]=jnp.where(ok,k1,k1[W1:W1+1,:]).astype(jnp.bfloat16)
        v1=kv_ref[pl.ds(start,ROWS),DH:2*DH].astype(jnp.float32)
        v1=jnp.where(ok,v1,0.0)
        v1t[0:DH,:]=v1.T.astype(jnp.bfloat16)
        v1t[DH:,:]=(lax.broadcasted_iota(jnp.int32,(VR-DH,ROWS),1)>=inv).astype(jnp.float32).astype(jnp.bfloat16)
        k2=kv_ref[pl.ds(start+W1-W2,2*QB),2*DH:3*DH].astype(jnp.float32)
        v2=kv_ref[pl.ds(start+W1-W2,2*QB),3*DH:4*DH].astype(jnp.float32)
        row2=lax.broadcasted_iota(jnp.int32,(2*QB,DH),0)
        ok2=(inv<W1)|(row2>=W2)
        k2f[...]=jnp.where(ok2,k2,k2[W2:W2+1,:])
        v2=jnp.where(ok2,v2,0.0)
        v2x=jnp.concatenate([v2.T,(lax.broadcasted_iota(jnp.int32,(VR-DH,2*QB),1)>=jnp.where(inv<W1,0,W2)).astype(jnp.float32)],axis=0).astype(jnp.bfloat16)
        for c in range(NCH):
            v2e[c]=jnp.dot(v2x,e_ref[:,c*CH*lanes:(c+1)*CH*lanes],preferred_element_type=jnp.float32)
    scale=LOG2E/np.sqrt(DH)
    for h in range(HG):
        qs[h*QB:(h+1)*QB,:]=q_ref[:,h*DH:(h+1)*DH].astype(jnp.float32)*scale
    tri=lax.broadcasted_iota(jnp.int32,(QB,CH*lanes),0)<=(lax.broadcasted_iota(jnp.int32,(QB,CH*lanes),1)%QB)

    def qk(c,slot):
        ps=[]
        for u in range(CH):
            k2=k2f[pl.ds(c*CH+u+1,QB),:]
            ps.append((qs[...].reshape(HG,QB,DH)*k2[None]).reshape(lanes,DH).astype(jnp.bfloat16))
        paired=jnp.concatenate(ps,axis=0)
        L=lax.dot_general(k1x[...],paired,(((1,),(1,)),((),())),preferred_element_type=jnp.float32)
        comb=jnp.where(tri,L[W1:],L[:QB])
        sbuf[slot,0:QB]=comb
        sbuf[slot,QB:]=L[QB:W1]
        cm=jnp.maximum(jnp.max(comb,axis=0,keepdims=True),jnp.max(L[QB:W1],axis=0,keepdims=True))
        r=cm[:,0:lanes]
        for u in range(1,CH): r=jnp.maximum(r,cm[:,u*lanes:(u+1)*lanes])
        return r

    def pv(c,slot,m_old,m_new):
        mm=jnp.concatenate([m_new]*CH,axis=1)
        p=jnp.exp2(sbuf[slot]-mm).astype(jnp.bfloat16)
        zero=jnp.zeros((QB,CH*lanes),jnp.bfloat16)
        pf=jnp.concatenate([jnp.where(tri,zero,p[:QB]),p[QB:],jnp.where(tri,p[:QB],zero)],axis=0)
        O=jnp.dot(v1t[...],pf,preferred_element_type=jnp.float32)
        w=O*v2e[c]
        r=w[:,0:lanes]
        for u in range(1,CH): r=r+w[:,u*lanes:(u+1)*lanes]
        acc[...]=acc[...]*jnp.exp2(m_old-m_new)+r

    acc[...]=jnp.zeros_like(acc)
    m0=qk(0,0)
    def step(t,carry):
        m_old,m_new=carry
        c=t*2
        m1=jnp.maximum(m_new,qk(c+1,1))
        pv(c,0,m_old,m_new)
        m2=jnp.maximum(m1,qk(jnp.minimum(c+2,NCH-1),0))
        pv(c+1,1,m_new,m1)
        return m1,m2
    lax.fori_loop(0,NCH//2,step,(m0,m0))
    a=acc[0:DH,:]/acc[DH:DH+1,:]
    lane=lax.broadcasted_iota(jnp.int32,(DH,lanes),1)//QB
    for h in range(HG):
        r=pltpu.roll(a,(b-h+HG)%HG*QB,1)
        i=pl.multiple_of((g*HG+h)*DH,DH)
        prev=out_ref[pl.ds(i,DH),:]
        out_ref[pl.ds(i,DH),:]=jnp.where(lane==b,r.astype(jnp.float32),prev.astype(jnp.float32)).astype(jnp.bfloat16)

def spread():
    lanes=HG*QB
    col=np.arange(W2*lanes); m=col//lanes; i=col%QB
    return (np.arange(2*QB)[:,None]==(i+m+1)[None,:])

def attention(queries, stacked, inval):
    T,HD=queries.shape
    nb=T//QB; ng=HD//(HG*DH)
    lanes=HG*QB
    E=jnp.asarray(spread(),jnp.bfloat16)
    full=lambda s: pl.BlockSpec(s,lambda b,g:(0,)*len(s))
    return pl.pallas_call(
        att_kernel,
        out_shape=jax.ShapeDtypeStruct((HD,T),jnp.bfloat16),
        grid=(nb,ng),
        in_specs=[pl.BlockSpec(memory_space=pltpu.SMEM),
                  pl.BlockSpec((QB,HG*DH),lambda b,g:(b,g)),
                  full(stacked.shape),full(E.shape)],
        out_specs=full((HD,T)),
        scratch_shapes=[pltpu.VMEM((ROWS,DH),jnp.bfloat16),pltpu.VMEM((VR,ROWS),jnp.bfloat16),
            pltpu.VMEM((NCH,VR,CH*lanes),jnp.float32),pltpu.VMEM((2*QB,DH),jnp.float32),
            pltpu.VMEM((lanes,DH),jnp.float32),pltpu.VMEM((2,W1,CH*lanes),jnp.float32),pltpu.VMEM((VR,lanes),jnp.float32)],
        compiler_params=pltpu.CompilerParams(vmem_limit_bytes=48*2**20),
    )(inval,queries,stacked,E)

HOPS = 3


def shifted(block, axis, distance):
    devices = range(lax.axis_size(axis))
    return lax.ppermute(block, axis, [(i - distance, i) for i in devices if i - distance in devices])


def rotated(block, axis, group, distance):
    devices = range(lax.axis_size(axis))
    return lax.ppermute(
        block, axis, [(i, i - i % group + (i % group + distance) % group) for i in devices]
    )


def collect_window(kv_rows, shards_back):
    held = kv_rows
    shard = kv_rows.shape[0]
    count = 1
    while count < shards_back + 1:
        number = min(count, shards_back + 1 - count)
        incoming = shifted(held[-number * shard :], "ctx", count)
        held = jnp.concatenate([incoming, held], axis=0)
        count += number
    return held


def body(queries, kv_rows, doc_start, destination, out_weight):
    position = lax.axis_index("ctx")
    tokens = queries.shape[0]
    blocks = tokens // QB
    group = HOPS + 1
    back = W1 // tokens
    stacked = collect_window(kv_rows, back)
    mine = position * blocks + jnp.arange(blocks, dtype=jnp.int32)
    inval = jnp.clip(doc_start[mine] - (mine * QB - W1), 0, W1).astype(jnp.int32)
    attended = attention(queries, stacked, inval)
    partial = lax.dot_general(
        out_weight, attended, (((0,), (0,)), ((), ())), preferred_element_type=jnp.float32
    )
    summed = lax.psum_scatter(partial, "head", scatter_dimension=0, tiled=True).astype(jnp.bfloat16)
    pieces = [summed] + [rotated(summed, "ctx", group, r) for r in range(1, group)]
    token = jnp.arange(tokens, dtype=jnp.int32)
    slots = mine[token // QB] * QB + token % QB
    picks = []
    for r in range(group):
        owner = position - position % group + (position % group - r + group) % group
        target = destination[owner * blocks + token // QB] * QB + token % QB
        picks.append(target[:, None] == slots[None, :])
    pick = jnp.concatenate(picks, axis=0).astype(jnp.bfloat16)
    return jnp.dot(
        jnp.concatenate(pieces, axis=1), pick, preferred_element_type=jnp.float32
    ).astype(jnp.bfloat16)


def solution(mesh):
    in_specs = (P("ctx", "head"), P("ctx", None), P(), P(), P("head", None))
    return jax.shard_map(
        body, mesh=mesh, in_specs=in_specs, out_specs=P("head", "ctx"), check_vma=False
    )
```

profile of v0, /device:TPU:0, one launch (start us, length us, event | category | flops | bytes accessed | tf_op | source)
XLA Modules:
  0.0 155.0 jit_solution(17289598724393244786)
XLA Ops:
  6.5 5.0 %collective-permute-start.1 = (bf16[128,512]{1,0:T(8,128)(2,1)}, bf16[128,512]{1,0:T(8,128)(2,1)S(1)}, u32[]{:S(2)}, u32[]{:S(2)}) collective-permute-start(bf16[128,512]{1,0:T(8,128)(2,1)} %param.7), channel_id=1, source_target_pairs={{0,2},{2,4},{4,6},{6,8},{8,10},{10,12},{12,14},{14,16},{16,18},{18... | collective-permute-start | bytes 393224 | tf_op jit(solution)/shard_map/ppermute | solution.py:120
  11.5 3.5 %collective-permute-start = (bf16[128,512]{1,0:T(8,128)(2,1)}, bf16[128,512]{1,0:T(8,128)(2,1)S(1)}, u32[]{:S(2)}, u32[]{:S(2)}) collective-permute-start(bf16[128,512]{1,0:T(8,128)(2,1)} %param.7), channel_id=1, source_target_pairs={{0,8},{2,10},{4,12},{6,14},{8,16},{10,18},{12,20},{14,22},{16,24},... | collective-permute-start | bytes 393224 | tf_op jit(solution)/shard_map/ppermute | solution.py:120
  15.1 0.9 pad_maximum_fusion.1
  16.0 4.7 %collective-permute-start.2 = (bf16[256,512]{1,0:T(8,128)(2,1)S(1)}, bf16[256,512]{1,0:T(8,128)(2,1)S(1)}, u32[]{:S(2)}, u32[]{:S(2)}) collective-permute-start(bf16[256,512]{1,0:T(8,128)(2,1)S(1)} %pad_maximum_fusion.1), channel_id=1, source_target_pairs={{0,4},{2,6},{4,8},{6,10},{8,12},{10,14},{12,16},{14,18},{16,20},{1... | collective-permute-start | bytes 786440 | tf_op jit(solution)/shard_map/ppermute | solution.py:120
  20.8 1.3 gather_fusion
  22.1 3.3 %collective-permute-done.2 = bf16[256,512]{1,0:T(8,128)(2,1)S(1)} collective-permute-done((bf16[256,512]{1,0:T(8,128)(2,1)S(1)}, bf16[256,512]{1,0:T(8,128)(2,1)S(1)}, u32[]{:S(2)}, u32[]{:S(2)}) %collective-permute-start.2) | collective-permute-done | bytes 262176 | tf_op jit(solution)/shard_map/ppermute | solution.py:120
  25.4 0.9 pad_maximum_fusion.kv_ref
  26.4 86.4 %shard_map.64 = bf16[2048,128]{1,0:T(8,128)(2,1)S(1)} custom-call(s32[4]{0:T(128)S(1)} %subtract_clamp_fusion.inval_ref, bf16[128,2048]{1,0:T(8,128)(2,1)S(1)} %copy-done.1, bf16[640,512]{1,0:T(8,128)(2,1)S(1)} %pad_maximum_fusion.kv_ref, bf16[64,4096]{1,0:T(8,128)(2,1)S(1)} %copy-done.2), custom_call_target="tpu_custom_call" | custom-call | tf_op jit(solution)/shard_map/pallas_call | solution.py:101
  112.8 5.7 %convolution_bitcast_fusion = f32[2048,128]{0,1:T(8,128)} fusion(bf16[2048,128]{1,0:T(8,128)(2,1)S(1)} %shard_map.64, bf16[2048,2048]{1,0:T(8,128)(2,1)} %param.10), kind=kOutput, calls=%fused_computation.5 | convolution fusion | flops 1073741824 | bytes 9961472 | tf_op jit(solution)/shard_map/dot_general | solution.py:152
  118.5 1.2 gather_fusion.4
  119.8 1.2 gather_fusion.1
  121.1 1.2 gather_fusion.3
  122.4 1.2 gather_fusion.2
  123.6 0.6 fusion.24
  124.2 2.5 %fusion.16 = (s32[128]{0:T(128)S(1)}, s32[128]{0:T(128)S(1)}) fusion(s32[]{:T(128)} %bitcast.3, s32[]{:T(128)} %bitcast.4, s32[]{:T(128)} %bitcast.6, s32[]{:T(128)} %bitcast.5, s32[128]{0:T(128)S(1)} %gather_fusion.4), kind=kLoop, calls=%fused_computation.48 | loop fusion | flops 3456 | bytes 1552 | tf_op jit(solution)/shard_map/add | solution.py:158
  126.7 2.6 %reduce-scatter.2.cloned.1.call-done = f32[1024,128]{0,1:T(8,128)} async-done(((f32[2048,128]{0,1:T(8,128)}), f32[1024,128]{0,1:T(8,128)}) %reduce-scatter.2.cloned.1.call-update) | async-done | bytes 524304 | tf_op jit(solution)/shard_map/reduce_scatter | solution.py:155
  129.4 1.1 convert_element_type.7
  130.4 2.7 %collective-permute-start.5 = (bf16[1024,128]{0,1:T(8,128)(2,1)S(1)}, bf16[1024,128]{0,1:T(8,128)(2,1)S(1)}, u32[]{:S(2)}, u32[]{:S(2)}) collective-permute-start(bf16[1024,128]{0,1:T(8,128)(2,1)S(1)} %convert_element_type.7), channel_id=1, source_target_pairs={{0,6},{2,0},{4,2},{6,4},{8,14},{10,8},{12,10},{14,12},{16,22},{18,... | collective-permute-start | bytes 786440 | tf_op jit(solution)/shard_map/ppermute | solution.py:125
  133.1 0.6 collective-permute-start.4
  133.7 0.6 collective-permute-start.3
  134.3 0.1 broadcast_compare_fusion.3
  134.4 5.4 %collective-permute-done.5 = bf16[1024,128]{0,1:T(8,128)(2,1)S(1)} collective-permute-done((bf16[1024,128]{0,1:T(8,128)(2,1)S(1)}, bf16[1024,128]{0,1:T(8,128)(2,1)S(1)}, u32[]{:S(2)}, u32[]{:S(2)}) %collective-permute-start.5) | collective-permute-done | bytes 262176 | tf_op jit(solution)/shard_map/ppermute | solution.py:125
  139.8 7.2 %collective-permute-done.4 = bf16[1024,128]{0,1:T(8,128)(2,1)S(1)} collective-permute-done((bf16[1024,128]{0,1:T(8,128)(2,1)S(1)}, bf16[1024,128]{0,1:T(8,128)(2,1)S(1)}, u32[]{:S(2)}, u32[]{:S(2)}) %collective-permute-start.4) | collective-permute-done | bytes 262176 | tf_op jit(solution)/shard_map/ppermute | solution.py:125
  147.0 1.2 convolution_convert_fusion
  (25 shorter events, 0.1 us)
Async XLA Ops:
  6.5 112.0 %copy-start = (s32[64]{0:T(128)S(1)}, s32[64]{0:T(128)}, u32[]{:S(2)}) copy-start(s32[64]{0:T(128)} %param.9) | copy-start | bytes 772
  6.5 19.8 %copy-start.2 = (bf16[64,4096]{1,0:T(8,128)(2,1)S(1)}, bf16[64,4096]{1,0:T(8,128)(2,1)}, u32[]{:S(2)}) copy-start(bf16[64,4096]{1,0:T(8,128)(2,1)} %constant.136.clone.e_ref) | copy-start | bytes 1572868
  6.5 19.8 %copy-start.1 = (bf16[128,2048]{1,0:T(8,128)(2,1)S(1)}, bf16[128,2048]{1,0:T(8,128)(2,1)}, u32[]{:S(2)}) copy-start(bf16[128,2048]{1,0:T(8,128)(2,1)} %q_ref.1) | copy-start | bytes 1572868
  6.5 122.8 %reduce-scatter.2.cloned.1.call-start = ((), (), s32[]{:S(2)}) async-start(), calls=%async_computation.1 | async-start | bytes 1572864 | tf_op jit(solution)/shard_map/reduce_scatter | solution.py:155
  6.5 8.5 %collective-permute-start.1 = (bf16[128,512]{1,0:T(8,128)(2,1)}, bf16[128,512]{1,0:T(8,128)(2,1)S(1)}, u32[]{:S(2)}, u32[]{:S(2)}) collective-permute-start(bf16[128,512]{1,0:T(8,128)(2,1)} %param.7), channel_id=1, source_target_pairs={{0,2},{2,4},{4,6},{6,8},{8,10},{10,12},{12,14},{14,16},{16,18},{18... | collective-permute-start | bytes 393224 | tf_op jit(solution)/shard_map/ppermute | solution.py:120
  11.5 10.5 %collective-permute-start = (bf16[128,512]{1,0:T(8,128)(2,1)}, bf16[128,512]{1,0:T(8,128)(2,1)S(1)}, u32[]{:S(2)}, u32[]{:S(2)}) collective-permute-start(bf16[128,512]{1,0:T(8,128)(2,1)} %param.7), channel_id=1, source_target_pairs={{0,8},{2,10},{4,12},{6,14},{8,16},{10,18},{12,20},{14,22},{16,24},... | collective-permute-start | bytes 393224 | tf_op jit(solution)/shard_map/ppermute | solution.py:120
  16.0 9.4 %collective-permute-start.2 = (bf16[256,512]{1,0:T(8,128)(2,1)S(1)}, bf16[256,512]{1,0:T(8,128)(2,1)S(1)}, u32[]{:S(2)}, u32[]{:S(2)}) collective-permute-start(bf16[256,512]{1,0:T(8,128)(2,1)S(1)} %pad_maximum_fusion.1), channel_id=1, source_target_pairs={{0,4},{2,6},{4,8},{6,10},{8,12},{10,14},{12,16},{14,18},{16,20},{1... | collective-permute-start | bytes 786440 | tf_op jit(solution)/shard_map/ppermute | solution.py:120
  130.4 9.4 %collective-permute-start.5 = (bf16[1024,128]{0,1:T(8,128)(2,1)S(1)}, bf16[1024,128]{0,1:T(8,128)(2,1)S(1)}, u32[]{:S(2)}, u32[]{:S(2)}) collective-permute-start(bf16[1024,128]{0,1:T(8,128)(2,1)S(1)} %convert_element_type.7), channel_id=1, source_target_pairs={{0,6},{2,0},{4,2},{6,4},{8,14},{10,8},{12,10},{14,12},{16,22},{18,... | collective-permute-start | bytes 786440 | tf_op jit(solution)/shard_map/ppermute | solution.py:125
  133.1 13.9 %collective-permute-start.4 = (bf16[1024,128]{0,1:T(8,128)(2,1)S(1)}, bf16[1024,128]{0,1:T(8,128)(2,1)S(1)}, u32[]{:S(2)}, u32[]{:S(2)}) collective-permute-start(bf16[1024,128]{0,1:T(8,128)(2,1)S(1)} %convert_element_type.7), channel_id=1, source_target_pairs={{0,4},{2,6},{4,0},{6,2},{8,12},{10,14},{12,8},{14,10},{16,20},{18,... | collective-permute-start | bytes 786440 | tf_op jit(solution)/shard_map/ppermute | solution.py:125
  133.7 13.3 %collective-permute-start.3 = (bf16[1024,128]{0,1:T(8,128)(2,1)S(1)}, bf16[1024,128]{0,1:T(8,128)(2,1)S(1)}, u32[]{:S(2)}, u32[]{:S(2)}) collective-permute-start(bf16[1024,128]{0,1:T(8,128)(2,1)S(1)} %convert_element_type.7), channel_id=1, source_target_pairs={{0,2},{2,4},{4,6},{6,0},{8,10},{10,12},{12,14},{14,8},{16,18},{18,... | collective-permute-start | bytes 786440 | tf_op jit(solution)/shard_map/ppermute | solution.py:125
Sparse Core Ops, SparseCore 0:
  118.6 10.7 reduce-scatter.1
where the time goes:
time: 155 us
  Pallas kernels  86.4 us (56%)
  waiting for transfers between devices  18.6 us (12%)
  starting transfers between devices  17 us (11%)
  between operations  13.7 us (9%)
  matrix products  6.85 us (4%)
  local copies, waits for them, and re-layouts  6.81 us (4%)
  other arithmetic  5.7 us (4%)
    pallas_call x1, Pallas kernels, attention(): pl.pallas_call(att_kernel, out_shape=jax.ShapeDtypeStruct((HD, T), jnp.bf...  86.4 us
    ppermute x3, starting transfers between devices, shifted(): lax.ppermute(block, axis, [(i - distance, i) for i in devices if i - dist...  13.2 us
    ppermute x3, waiting for transfers between devices, rotated(): lax.ppermute(block, axis, [(i, i - i % group + (i % group + distance) % g...  12.6 us
    dot_general x1, matrix products, body(): lax.dot_general(out_weight, attended, (((0,), (0,)), ((), ())), preferred...  5.66 us
    gather x4, local copies, waits for them, and re-layouts, body(): target = destination[owner * blocks + token // QB] * QB + token % QB  4.91 us
    ppermute x3, starting transfers between devices, rotated(): lax.ppermute(block, axis, [(i, i - i % group + (i % group + distance) % g...  3.81 us
    ppermute x3, waiting for transfers between devices, shifted(): lax.ppermute(block, axis, [(i - distance, i) for i in devices if i - dist...  3.34 us
  transfers between devices with their start and end apart: 7, of which 4 were waited for; matrix products, arithmetic and copies ran while one was open for 7% of the time, Pallas kernels for 0%

commit v1 on v0

v1 whole, which is shorter than its diff:
```python
import jax
import jax.numpy as jnp
import numpy as np
from jax import lax
from jax.experimental import pallas as pl
from jax.experimental.pallas import tpu as pltpu
from jax.sharding import PartitionSpec as P

DH = 128
W1 = 512
W2 = 32
QB = 32
LANES = 128
PACK = 16
VR = DH + PACK
UNROLL = 8
LOG2E = 1.4426950408889634


def attention_kernel(inval_ref, q_ref, kv_ref, out_ref, k1n, k1s, v1t, v1n, k2x, v2x, rowid, laneid, q3, sbuf, peak, part, top2, att, rows):
    tokens = q_ref.shape[0]
    heads = q_ref.shape[1] // DH
    cols = W2 * heads
    per_tile = LANES // heads
    tiles = tokens // LANES
    near_tiles = cols // LANES
    size = max(heads, PACK)
    per_pack = size // heads
    scale = LOG2E / np.sqrt(DH)
    f32, bf16 = jnp.float32, jnp.bfloat16

    def iota(shape, dim):
        return lax.broadcasted_iota(jnp.int32, shape, dim)

    for h in range(heads):
        q3[pl.ds(h, tokens, stride=heads), :] = q_ref[:, h * DH : (h + 1) * DH].astype(f32)
    second = kv_ref[W1 - W2 :, 2 * DH : 3 * DH].astype(f32)
    second = jnp.broadcast_to(second[:, None, :], (tokens + W2, heads, DH))
    k2x[...] = second.reshape(k2x.shape).astype(bf16)
    k1n[...] = kv_ref[W1:, :DH]
    rowid[...] = iota(rowid.shape, 0).astype(f32).astype(bf16)
    laneid[...] = iota(laneid.shape, 1).astype(f32).astype(bf16)
    for k in range(tiles):
        own = kv_ref[W1 + k * LANES : W1 + (k + 1) * LANES, DH : 2 * DH]
        v1n[k, :DH] = own.astype(f32).T.astype(bf16)
        v1n[k, DH:] = jnp.ones((VR - DH, LANES), bf16)
    near = LANES + tokens
    v2t = kv_ref[W1 - LANES :, 3 * DH :].astype(f32).T
    v2t = jnp.concatenate([v2t, jnp.ones((VR - DH, near), f32)], axis=0).astype(bf16)
    first = LANES - W2
    for k in range((tokens + W2) // per_tile):
        pick = iota((near, LANES), 0) == first + k * per_tile + iota((near, LANES), 1) // heads
        v2x[k] = jnp.dot(v2t, pick.astype(f32).astype(bf16), preferred_element_type=f32)

    def reset(t, inv):
        kt = kv_ref[pl.ds(pl.multiple_of(W1 + t, PACK), PACK), :].astype(f32)[:1]
        window = kv_ref[:W1, : 2 * DH].astype(f32)
        ok = iota((W1, DH), 0) >= inv
        k1s[...] = jnp.where(ok, window[:, :DH], kt[:, :DH]).astype(bf16)
        values = jnp.where(ok, window[:, DH:], 0.0)
        for k in range(W1 // LANES):
            v1t[k, :DH] = values[k * LANES : (k + 1) * LANES].T.astype(bf16)
            live = k * LANES + iota((VR - DH, LANES), 1) >= inv
            v1t[k, DH:] = live.astype(f32).astype(bf16)
        k1n[...] = jnp.where(iota((tokens, DH), 0) < t, kt[:, :DH], k1n[...].astype(f32)).astype(bf16)
        for k in range(tiles):
            gone = k * LANES + iota((VR, LANES), 1) < t
            v1n[k] = jnp.where(gone, 0.0, v1n[k].astype(f32)).astype(bf16)

        @pl.when(inv == W1)
        def _():
            pack0 = t // per_pack
            fill = jnp.broadcast_to(kt[:, 2 * DH : 3 * DH], (size, DH)).astype(bf16)
            for s in range(W2 // per_pack):
                k2x[pack0 + s] = fill
            for k in range(near_tiles):
                v2x[t // per_tile + k] = jnp.zeros((VR, LANES), f32)

    def score(t, slot):
        mark = t.astype(f32).astype(bf16)
        keys = [
            jnp.where(rowid[...] + (k * LANES) <= mark, k1n[k * LANES : (k + 1) * LANES], k1s[k * LANES : (k + 1) * LANES])
            for k in range(tiles)
        ]
        keys = jnp.concatenate(keys + [k1s[tokens:]], axis=0)
        query = q3[pl.ds(t * heads, heads), :]
        if heads < PACK:
            query = jnp.concatenate([query] * per_pack, axis=0)
        query = query.astype(bf16)
        here = t % W2
        base = (t - here) // per_pack
        wide = min(2 * LANES, cols)
        best = None
        for n in range(0, cols, wide):
            paired = []
            for s in range(n // size, (n + wide) // size):
                if heads >= PACK:
                    near_keys = k2x[base + s + jnp.where(s <= here, W2, 0)]
                else:
                    token = s * per_pack + iota((size, DH), 0) // heads
                    after = k2x[base + s + W2 // per_pack].astype(f32)
                    near_keys = jnp.where(token <= here, after, k2x[base + s].astype(f32)).astype(bf16)
                paired.append(near_keys * query)
            paired = jnp.concatenate(paired, axis=0)
            logits = lax.dot_general(
                keys, paired, (((1,), (1,)), ((), ())), preferred_element_type=f32
            )
            sbuf[slot, :, n : n + wide] = logits
            top = jnp.max(logits, axis=0, keepdims=True)
            for u in range(0, wide, LANES):
                some = top[:, u : u + LANES]
                best = some if best is None else jnp.maximum(best, some)
        peak[slot] = jnp.broadcast_to(best * scale, (8, LANES))

    def mix(t, slot):
        mark = t.astype(f32).astype(bf16)
        values = [
            jnp.where(laneid[...] + (k * LANES) <= mark, v1n[k], v1t[k]) for k in range(tiles)
        ] + [v1t[k] for k in range(tiles, W1 // LANES)]
        here = t % W2
        base = (t - here) // per_tile
        place = iota((VR, LANES), 1) // heads
        top = peak[slot][:1]
        wide = min(2 * LANES, cols)
        total = jnp.zeros((VR, LANES), f32)
        for n in range(0, cols, wide):
            product = jnp.zeros((VR, wide), f32)
            for k in range(0, W1, 2 * LANES):
                some = sbuf[slot, k : k + 2 * LANES, n : n + wide]
                weights = jnp.exp2(some * scale - jnp.concatenate([top] * (wide // LANES), axis=1))
                two = jnp.concatenate(values[k // LANES : k // LANES + 2], axis=1)
                product = product + jnp.dot(two, weights.astype(bf16), preferred_element_type=f32)
            for u in range(0, wide, LANES):
                k = (n + u) // LANES
                second = jnp.where(
                    place + k * per_tile <= here, v2x[base + near_tiles + k], v2x[base + k]
                )
                total = total + product[:, u : u + LANES] * second
        part[slot] = total
        top2[slot] = peak[slot]

    def finish(t, slot):
        lane = iota((DH, LANES), 1)
        top = top2[slot]
        best = top
        shift = LANES // 2
        while shift >= heads:
            best = jnp.maximum(best, pltpu.roll(best, shift, 1))
            shift //= 2
        total = part[slot] * jnp.exp2(top - best)[:1]
        shift = LANES // 2
        while shift >= heads:
            total = total + pltpu.roll(total, shift, 1)
            shift //= 2
        value = total[:DH] * (1.0 / total[DH : DH + 1])
        tile = t // per_tile
        att[tile] = jnp.where(lane // heads == t % per_tile, value, att[tile])

    def block(b, _):
        inv = inval_ref[b]
        t0 = b * QB

        @pl.when((b == 0) | (inv == W1))
        def _():
            reset(t0, inv)
            score(t0, 0)

        def several(s, _):
            t = t0 + UNROLL * s
            for u in range(UNROLL):
                score(jnp.minimum(t + u + 1, tokens - 1), (u + 1) % 2)
                mix(t + u, u % 2)
                finish(jnp.maximum(t + u - 1, 0), (u + 1) % 2)
            return 0

        return lax.fori_loop(0, QB // UNROLL, several, 0)

    lax.fori_loop(0, tokens // QB, block, 0)
    finish(tokens - 1, (tokens - 1) % 2)
    for k in range(tokens // per_tile):
        rows[k * LANES : (k + 1) * LANES, :] = att[k].T
    for h in range(heads):
        out_ref[:, h * DH : (h + 1) * DH] = rows[pl.ds(h, tokens, stride=heads), :].astype(bf16)


def attention(queries, stacked, inval):
    tokens, width = queries.shape
    heads = width // DH
    cols = W2 * heads
    f32, bf16 = jnp.float32, jnp.bfloat16
    return pl.pallas_call(
        attention_kernel,
        out_shape=jax.ShapeDtypeStruct((tokens, width), bf16),
        in_specs=[
            pl.BlockSpec(memory_space=pltpu.SMEM),
            pl.BlockSpec(memory_space=pltpu.VMEM),
            pl.BlockSpec(memory_space=pltpu.VMEM),
        ],
        out_specs=pl.BlockSpec(memory_space=pltpu.VMEM),
        scratch_shapes=[
            pltpu.VMEM((tokens, DH), bf16),
            pltpu.VMEM((W1, DH), bf16),
            pltpu.VMEM((W1 // LANES, VR, LANES), bf16),
            pltpu.VMEM((tokens // LANES, VR, LANES), bf16),
            pltpu.VMEM(((tokens + W2) * heads // max(heads, PACK), max(heads, PACK), DH), bf16),
            pltpu.VMEM(((tokens + W2) * heads // LANES, VR, LANES), f32),
            pltpu.VMEM((LANES, DH), bf16),
            pltpu.VMEM((VR, LANES), bf16),
            pltpu.VMEM((tokens * heads, DH), f32),
            pltpu.VMEM((2, W1, cols), f32),
            pltpu.VMEM((2, 8, LANES), f32),
            pltpu.VMEM((2, VR, LANES), f32),
            pltpu.VMEM((2, 8, LANES), f32),
            pltpu.VMEM((tokens * heads // LANES, DH, LANES), f32),
            pltpu.VMEM((tokens * heads, DH), f32),
        ],
        compiler_params=pltpu.CompilerParams(vmem_limit_bytes=24 * 2**20),
    )(inval, queries, stacked)

HOPS = 3


def shifted(block, axis, distance):
    devices = range(lax.axis_size(axis))
    return lax.ppermute(block, axis, [(i - distance, i) for i in devices if i - distance in devices])


def swapped(block, axis, bits):
    return lax.ppermute(block, axis, [(i, i ^ bits) for i in range(lax.axis_size(axis))])


def summed_over_heads(partial):
    count = lax.axis_size("head")
    width = partial.shape[1] // count
    if count != 2:
        return lax.psum_scatter(partial, "head", scatter_dimension=1, tiled=True)
    here = lax.axis_index("head")
    theirs = lax.dynamic_slice_in_dim(partial, (1 - here) * width, width, 1)
    mine = lax.dynamic_slice_in_dim(partial, here * width, width, 1)
    return mine + swapped(theirs, "head", 1)


def body(queries, kv_rows, doc_start, destination, out_weight):
    position = lax.axis_index("ctx")
    tokens = queries.shape[0]
    blocks = tokens // QB
    group = HOPS + 1
    back = W1 // tokens
    stacked = jnp.concatenate(
        [shifted(kv_rows, "ctx", back - k) for k in range(back)] + [kv_rows], axis=0
    )
    first = position * blocks
    starts = lax.dynamic_slice_in_dim(doc_start, first, blocks, 0)
    own_rows = (first + jnp.arange(blocks, dtype=jnp.int32)) * QB
    inval = jnp.clip(starts - (own_rows - W1), 0, W1).astype(jnp.int32)
    place = position % group
    slots = group * blocks
    targets = lax.dynamic_slice_in_dim(destination, first - place * blocks, slots, 0)
    row = jnp.arange(group * tokens, dtype=jnp.int32)
    source = (place ^ (row // tokens)) * blocks + row % tokens // QB
    known = source[:, None] == jnp.arange(slots, dtype=jnp.int32)[None, :]
    target = jnp.sum(jnp.where(known, targets[None, :], 0), axis=1) * QB + row % QB
    pick = target[:, None] == (first * QB + jnp.arange(tokens, dtype=jnp.int32))[None, :]
    pick = pick.astype(jnp.bfloat16)
    attended = attention(queries, stacked, inval)
    partial = jnp.dot(attended, out_weight, preferred_element_type=jnp.float32)
    projected = summed_over_heads(partial).astype(jnp.bfloat16)
    pieces = jnp.concatenate(
        [projected] + [swapped(projected, "ctx", r) for r in range(1, group)], axis=0
    )
    return lax.dot_general(
        pieces, pick, (((0,), (0,)), ((), ())), preferred_element_type=jnp.float32
    ).astype(jnp.bfloat16)


def solution(mesh):
    in_specs = (P("ctx", "head"), P("ctx", None), P(), P(), P("head", None))
    return jax.shard_map(
        body, mesh=mesh, in_specs=in_specs, out_specs=P("head", "ctx"), check_vma=False
    )
```

time: 155 us -> 91.8 us (0.59)
  Pallas kernels: 86.4 us -> 45.8 us
  between operations: 13.7 us -> 0.18 us
  other arithmetic: 5.7 us -> 0.9 us
  local copies, waits for them, and re-layouts: 6.81 us -> 2.13 us
  starting transfers between devices: 17 us -> 21 us
  waiting for transfers between devices: 18.6 us -> 15.6 us
    pallas_call x1, Pallas kernels: 86.4 us -> 45.8 us  [attention(): pl.pallas_call(attention_kernel, out_shape=jax.ShapeDtypeStruct((tokens,...]
    gather x6 -> x0, local copies, waits for them, and re-layouts: 6.8 us -> none  [the longest x4 4.91 us: body(): target = destination[owner * blocks + token // QB] * QB + token % QB]
    reduce_scatter x1 -> x0, waiting for transfers between devices: 2.63 us -> none  [body(): lax.psum_scatter(partial, 'head', scatter_dimension=0, tiled=True)]
    add x4 -> x3, other arithmetic: 2.52 us -> 0.02 us  [the longest x1 0.01 us: body(): source = (place ^ row // tokens) * blocks + row % tokens // QB]
    ppermute x3 -> x4, starting transfers between devices: 13.2 us -> 15.2 us  [shifted(): lax.ppermute(block, axis, [(i - distance, i) for i in devices if i - dist...]
    ppermute x3 -> x4, starting transfers between devices: 3.81 us -> 5.74 us  [swapped(): lax.ppermute(block, axis, [(i, i ^ bits) for i in range(lax.axis_size(axi...]
    concatenate x2 -> x0, other arithmetic: 1.89 us -> none  [collect_window(): held = jnp.concatenate([incoming, held], axis=0)]
    ppermute x3 -> x4, waiting for transfers between devices: 3.34 us -> 2 us  [shifted(): lax.ppermute(block, axis, [(i - distance, i) for i in devices if i - dist...]
  transfers between devices with their start and end apart: 7 -> 8, of which waited for: 4 -> 5; matrix products, arithmetic and copies ran while one was open for 7% -> 1% of each run, Pallas kernels for 0% -> 0%
where the time goes in v1:
time: 91.8 us; the launch traced here: 91.5 us
  Pallas kernels  45.8 us (50%)
  starting transfers between devices  21 us (23%)
  waiting for transfers between devices  15.6 us (17%)
  matrix products  5.94 us (6%)
  local copies, waits for them, and re-layouts  2.13 us (2%)
    pallas_call x1, Pallas kernels, attention(): pl.pallas_call(attention_kernel, out_shape=jax.ShapeDtypeStruct((tokens,...  45.8 us
    ppermute x4, starting transfers between devices, shifted(): lax.ppermute(block, axis, [(i - distance, i) for i in devices if i - dist...  15.2 us
    ppermute x4, waiting for transfers between devices, swapped(): lax.ppermute(block, axis, [(i, i ^ bits) for i in range(lax.axis_size(axi...  13.6 us
    ppermute x4, starting transfers between devices, swapped(): lax.ppermute(block, axis, [(i, i ^ bits) for i in range(lax.axis_size(axi...  5.74 us
    dot_general x1, matrix products, body(): partial = jnp.dot(attended, out_weight, preferred_element_type=jnp.float32)  4.67 us
    ppermute x4, waiting for transfers between devices, shifted(): lax.ppermute(block, axis, [(i - distance, i) for i in devices if i - dist...  2 us
  transfers between devices with their start and end apart: 8, of which 5 were waited for; matrix products, arithmetic and copies ran while one was open for 1% of the time, Pallas kernels for 0%

profile of v1, /device:TPU:0, one launch (start us, length us, event | category | flops | bytes accessed | tf_op | source)
XLA Modules:
  0.0 91.5 jit_solution(5148511437062181317)
XLA Ops:
  0.0 4.9 %collective-permute-start = (bf16[128,512]{1,0:T(8,128)(2,1)}, bf16[128,512]{1,0:T(8,128)(2,1)S(1)}, u32[]{:S(2)}, u32[]{:S(2)}) collective-permute-start(bf16[128,512]{1,0:T(8,128)(2,1)} %param.6), channel_id=1, source_target_pairs={{0,8},{2,10},{4,12},{6,14},{8,16},{10,18},{12,20},{14,22},{16,24},... | collective-permute-start | bytes 393224 | tf_op jit(solution)/shard_map/ppermute | solution.py:225
  4.9 4.4 %collective-permute-start.1 = (bf16[128,512]{1,0:T(8,128)(2,1)}, bf16[128,512]{1,0:T(8,128)(2,1)S(1)}, u32[]{:S(2)}, u32[]{:S(2)}) collective-permute-start(bf16[128,512]{1,0:T(8,128)(2,1)} %param.6), channel_id=1, source_target_pairs={{0,6},{2,8},{4,10},{6,12},{8,14},{10,16},{12,18},{14,20},{16,22},{... | collective-permute-start | bytes 393224 | tf_op jit(solution)/shard_map/ppermute | solution.py:225
  9.3 3.4 %collective-permute-start.2 = (bf16[128,512]{1,0:T(8,128)(2,1)}, bf16[128,512]{1,0:T(8,128)(2,1)S(1)}, u32[]{:S(2)}, u32[]{:S(2)}) collective-permute-start(bf16[128,512]{1,0:T(8,128)(2,1)} %param.6), channel_id=1, source_target_pairs={{0,4},{2,6},{4,8},{6,10},{8,12},{10,14},{12,16},{14,18},{16,20},{1... | collective-permute-start | bytes 393224 | tf_op jit(solution)/shard_map/ppermute | solution.py:225
  12.7 2.5 %collective-permute-start.3 = (bf16[128,512]{1,0:T(8,128)(2,1)}, bf16[128,512]{1,0:T(8,128)(2,1)S(1)}, u32[]{:S(2)}, u32[]{:S(2)}) collective-permute-start(bf16[128,512]{1,0:T(8,128)(2,1)} %param.6), channel_id=1, source_target_pairs={{0,2},{2,4},{4,6},{6,8},{8,10},{10,12},{12,14},{14,16},{16,18},{18... | collective-permute-start | bytes 393224 | tf_op jit(solution)/shard_map/ppermute | solution.py:225
  15.3 0.7 subtract_clamp_fusion.inval_ref
  16.1 2.0 %collective-permute-done.3 = bf16[128,512]{1,0:T(8,128)(2,1)S(1)} collective-permute-done((bf16[128,512]{1,0:T(8,128)(2,1)}, bf16[128,512]{1,0:T(8,128)(2,1)S(1)}, u32[]{:S(2)}, u32[]{:S(2)}) %collective-permute-start.3) | collective-permute-done | bytes 131104 | tf_op jit(solution)/shard_map/ppermute | solution.py:225
  18.1 0.9 %constant_dynamic-update-slice_fusion.kv_ref = bf16[640,512]{1,0:T(8,128)(2,1)S(1)} fusion(bf16[640,512]{1,0:T(8,128)(2,1)S(1)} %constant_dynamic-update-slice_fusion.1, bf16[128,512]{1,0:T(8,128)(2,1)} %param.6), kind=kLoop, calls=%fused_computation.14 | loop fusion | bytes 262144 | tf_op jit(solution)/shard_map/concatenate | solution.py:249
  19.0 1.0 %copy-done = bf16[128,2048]{1,0:T(8,128)(2,1)S(1)} copy-done((bf16[128,2048]{1,0:T(8,128)(2,1)S(1)}, bf16[128,2048]{1,0:T(8,128)(2,1)}, u32[]{:S(2)}) %copy-start) | copy-done | bytes 524312
  20.0 45.8 %shard_map.55 = bf16[128,2048]{1,0:T(8,128)(2,1)S(1)} custom-call(s32[4]{0:T(128)S(1)} %subtract_clamp_fusion.inval_ref, bf16[128,2048]{1,0:T(8,128)(2,1)S(1)} %copy-done, bf16[640,512]{1,0:T(8,128)(2,1)S(1)} %constant_dynamic-update-slice_fusion.kv_ref), custom_call_target="tpu_custom_call" | custom-call | tf_op jit(solution)/shard_map/pallas_call | solution.py:191
  65.9 0.0 copy-start.1
  65.9 4.7 %fusion.27 = f32[128,2048]{1,0:T(8,128)S(1)} fusion(bf16[128,2048]{1,0:T(8,128)(2,1)S(1)} %shard_map.55, bf16[2048,2048]{1,0:T(8,128)(2,1)} %param.9), kind=kOutput, calls=%fused_computation.50 | convolution fusion | flops 1073741824 | bytes 9961472 | tf_op jit(solution)/shard_map/dot_general | solution.py:266
  70.6 0.1 constant_dynamic-slice_fusion
  70.6 0.1 collective-permute-start.4
  70.7 0.1 dynamic_slice.15
  70.8 0.1 select_reduce_fusion
  70.9 1.7 %collective-permute-done.4 = f32[128,1024]{1,0:T(8,128)S(1)} collective-permute-done((f32[128,1024]{1,0:T(8,128)S(1)}, f32[128,1024]{1,0:T(8,128)S(1)}, u32[]{:S(2)}, u32[]{:S(2)}) %collective-permute-start.4) | collective-permute-done | bytes 524320 | tf_op jit(solution)/shard_map/ppermute | solution.py:229
  72.6 0.1 add_convert_fusion
  72.7 2.4 %collective-permute-start.5 = (bf16[128,1024]{1,0:T(8,128)(2,1)S(1)}, bf16[128,1024]{1,0:T(8,128)(2,1)S(1)}, u32[]{:S(2)}, u32[]{:S(2)}) collective-permute-start(bf16[128,1024]{1,0:T(8,128)(2,1)S(1)} %add_convert_fusion), channel_id=1, source_target_pairs={{0,2},{2,0},{4,6},{6,4},{8,10},{10,8},{12,14},{14,12},{16,18},{18,... | collective-permute-start | bytes 786440 | tf_op jit(solution)/shard_map/ppermute | solution.py:229
  75.1 1.9 %collective-permute-start.6 = (bf16[128,1024]{1,0:T(8,128)(2,1)S(1)}, bf16[128,1024]{1,0:T(8,128)(2,1)S(1)}, u32[]{:S(2)}, u32[]{:S(2)}) collective-permute-start(bf16[128,1024]{1,0:T(8,128)(2,1)S(1)} %add_convert_fusion), channel_id=1, source_target_pairs={{0,4},{2,6},{4,0},{6,2},{8,12},{10,14},{12,8},{14,10},{16,20},{18,... | collective-permute-start | bytes 786440 | tf_op jit(solution)/shard_map/ppermute | solution.py:229
  77.0 1.4 %collective-permute-start.7 = (bf16[128,1024]{1,0:T(8,128)(2,1)S(1)}, bf16[128,1024]{1,0:T(8,128)(2,1)S(1)}, u32[]{:S(2)}, u32[]{:S(2)}) collective-permute-start(bf16[128,1024]{1,0:T(8,128)(2,1)S(1)} %add_convert_fusion), channel_id=1, source_target_pairs={{0,6},{2,4},{4,2},{6,0},{8,14},{10,12},{12,10},{14,8},{16,22},{18,... | collective-permute-start | bytes 786440 | tf_op jit(solution)/shard_map/ppermute | solution.py:229
  78.3 3.8 %collective-permute-done.5 = bf16[128,1024]{1,0:T(8,128)(2,1)S(1)} collective-permute-done((bf16[128,1024]{1,0:T(8,128)(2,1)S(1)}, bf16[128,1024]{1,0:T(8,128)(2,1)S(1)}, u32[]{:S(2)}, u32[]{:S(2)}) %collective-permute-start.5) | collective-permute-done | bytes 262176 | tf_op jit(solution)/shard_map/ppermute | solution.py:229
  82.2 6.2 %collective-permute-done.6 = bf16[128,1024]{1,0:T(8,128)(2,1)S(1)} collective-permute-done((bf16[128,1024]{1,0:T(8,128)(2,1)S(1)}, bf16[128,1024]{1,0:T(8,128)(2,1)S(1)}, u32[]{:S(2)}, u32[]{:S(2)}) %collective-permute-start.6) | collective-permute-done | bytes 262176 | tf_op jit(solution)/shard_map/ppermute | solution.py:229
  88.4 1.8 %collective-permute-done.7 = bf16[128,1024]{1,0:T(8,128)(2,1)S(1)} collective-permute-done((bf16[128,1024]{1,0:T(8,128)(2,1)S(1)}, bf16[128,1024]{1,0:T(8,128)(2,1)S(1)}, u32[]{:S(2)}, u32[]{:S(2)}) %collective-permute-start.7) | collective-permute-done | bytes 262176 | tf_op jit(solution)/shard_map/ppermute | solution.py:229
  90.3 1.3 %convolution_convert_fusion = bf16[1024,128]{1,0:T(8,128)(2,1)} fusion(bf16[128,1024]{1,0:T(8,128)(2,1)S(1)} %collective-permute-done.7, bf16[128,1024]{1,0:T(8,128)(2,1)S(1)} %collective-permute-done.6, bf16[128,1024]{1,0:T(8,128)(2,1)S(1)} %collective-permute-done.5, bf16[128,1024]{1,0:T(8,128)(2,1)S(1)} %add_convert_fusion, s32[128]{0:T(128)S(1)} %iota_add_fusion, ...), kind=kOutput, calls=%fused_computation | convolution fusion | flops 138608640 | bytes 1313280 | tf_op jit(solution)/shard_map/dot_general | solution.py:271
  (12 shorter events, 0.1 us)
Async XLA Ops:
  0.0 16.0 %collective-permute-start = (bf16[128,512]{1,0:T(8,128)(2,1)}, bf16[128,512]{1,0:T(8,128)(2,1)S(1)}, u32[]{:S(2)}, u32[]{:S(2)}) collective-permute-start(bf16[128,512]{1,0:T(8,128)(2,1)} %param.6), channel_id=1, source_target_pairs={{0,8},{2,10},{4,12},{6,14},{8,16},{10,18},{12,20},{14,22},{16,24},... | collective-permute-start | bytes 393224 | tf_op jit(solution)/shard_map/ppermute | solution.py:225
  4.9 11.1 %collective-permute-start.1 = (bf16[128,512]{1,0:T(8,128)(2,1)}, bf16[128,512]{1,0:T(8,128)(2,1)S(1)}, u32[]{:S(2)}, u32[]{:S(2)}) collective-permute-start(bf16[128,512]{1,0:T(8,128)(2,1)} %param.6), channel_id=1, source_target_pairs={{0,6},{2,8},{4,10},{6,12},{8,14},{10,16},{12,18},{14,20},{16,22},{... | collective-permute-start | bytes 393224 | tf_op jit(solution)/shard_map/ppermute | solution.py:225
  9.3 6.7 %collective-permute-start.2 = (bf16[128,512]{1,0:T(8,128)(2,1)}, bf16[128,512]{1,0:T(8,128)(2,1)S(1)}, u32[]{:S(2)}, u32[]{:S(2)}) collective-permute-start(bf16[128,512]{1,0:T(8,128)(2,1)} %param.6), channel_id=1, source_target_pairs={{0,4},{2,6},{4,8},{6,10},{8,12},{10,14},{12,16},{14,18},{16,20},{1... | collective-permute-start | bytes 393224 | tf_op jit(solution)/shard_map/ppermute | solution.py:225
  12.7 5.3 %collective-permute-start.3 = (bf16[128,512]{1,0:T(8,128)(2,1)}, bf16[128,512]{1,0:T(8,128)(2,1)S(1)}, u32[]{:S(2)}, u32[]{:S(2)}) collective-permute-start(bf16[128,512]{1,0:T(8,128)(2,1)} %param.6), channel_id=1, source_target_pairs={{0,2},{2,4},{4,6},{6,8},{8,10},{10,12},{12,14},{14,16},{16,18},{18... | collective-permute-start | bytes 393224 | tf_op jit(solution)/shard_map/ppermute | solution.py:225
  19.0 1.0 %copy-start = (bf16[128,2048]{1,0:T(8,128)(2,1)S(1)}, bf16[128,2048]{1,0:T(8,128)(2,1)}, u32[]{:S(2)}) copy-start(bf16[128,2048]{1,0:T(8,128)(2,1)} %q_ref.1) | copy-start | bytes 1572868
  65.9 4.9 %copy-start.1 = (s32[64]{0:T(128)S(1)}, s32[64]{0:T(128)}, u32[]{:S(2)}) copy-start(s32[64]{0:T(128)} %param.8) | copy-start | bytes 772
  70.6 2.0 %collective-permute-start.4 = (f32[128,1024]{1,0:T(8,128)S(1)}, f32[128,1024]{1,0:T(8,128)S(1)}, u32[]{:S(2)}, u32[]{:S(2)}) collective-permute-start(f32[128,1024]{1,0:T(8,128)S(1)} %constant_dynamic-slice_fusion), channel_id=1, source_target_pairs={{0,1},{1,0},{2,3},{3,2},{4,5},{5,4},{6,7},{7,6},{8,9},{9,8},{10,11... | collective-permute-start | bytes 1572872 | tf_op jit(solution)/shard_map/ppermute | solution.py:229
  72.7 9.5 %collective-permute-start.5 = (bf16[128,1024]{1,0:T(8,128)(2,1)S(1)}, bf16[128,1024]{1,0:T(8,128)(2,1)S(1)}, u32[]{:S(2)}, u32[]{:S(2)}) collective-permute-start(bf16[128,1024]{1,0:T(8,128)(2,1)S(1)} %add_convert_fusion), channel_id=1, source_target_pairs={{0,2},{2,0},{4,6},{6,4},{8,10},{10,8},{12,14},{14,12},{16,18},{18,... | collective-permute-start | bytes 786440 | tf_op jit(solution)/shard_map/ppermute | solution.py:229
  75.1 13.3 %collective-permute-start.6 = (bf16[128,1024]{1,0:T(8,128)(2,1)S(1)}, bf16[128,1024]{1,0:T(8,128)(2,1)S(1)}, u32[]{:S(2)}, u32[]{:S(2)}) collective-permute-start(bf16[128,1024]{1,0:T(8,128)(2,1)S(1)} %add_convert_fusion), channel_id=1, source_target_pairs={{0,4},{2,6},{4,0},{6,2},{8,12},{10,14},{12,8},{14,10},{16,20},{18,... | collective-permute-start | bytes 786440 | tf_op jit(solution)/shard_map/ppermute | solution.py:229
  77.0 13.3 %collective-permute-start.7 = (bf16[128,1024]{1,0:T(8,128)(2,1)S(1)}, bf16[128,1024]{1,0:T(8,128)(2,1)S(1)}, u32[]{:S(2)}, u32[]{:S(2)}) collective-permute-start(bf16[128,1024]{1,0:T(8,128)(2,1)S(1)} %add_convert_fusion), channel_id=1, source_target_pairs={{0,6},{2,4},{4,2},{6,0},{8,14},{10,12},{12,10},{14,8},{16,22},{18,... | collective-permute-start | bytes 786440 | tf_op jit(solution)/shard_map/ppermute | solution.py:229

commit v2 on v1

v2 whole, which is shorter than its diff:
```python
import functools

import jax
import jax.numpy as jnp
import numpy as np
from jax import lax
from jax.experimental import pallas as pl
from jax.experimental.pallas import tpu as pltpu
from jax.sharding import PartitionSpec as P

DH = 128
W1 = 512
W2 = 32
QB = 32
LANES = 128
PACK = 16
VR = DH + PACK
SAMPLE = 32
AHEAD = 3
LIMIT = 1e30
LOG2E = 1.4426950408889634


def attention_kernel(pairs, outputs, meta_ref, q_ref, w_ref, *refs):
    shards, refs = refs[:pairs], refs[pairs:]
    out_refs, refs = refs[:outputs], refs[outputs:]
    kv_ref, wbuf, wsem, k1n, k1s, v1t, v1n, k2x, v2x, rowid, laneid, q3, part, top2, bad, rows = refs
    tokens = q_ref.shape[0]
    heads = q_ref.shape[1] // DH
    cols = W2 * heads
    group = LANES // heads
    tiles = tokens // LANES
    near_tiles = cols // LANES
    size = max(heads, PACK)
    pack = size // heads
    wide = min(2 * LANES, cols)
    scale = LOG2E / np.sqrt(DH)
    f32, bf16 = jnp.float32, jnp.bfloat16

    def iota(shape, dim):
        return lax.broadcasted_iota(jnp.int32, shape, dim)

    def either(cond, a, b):
        if isinstance(cond, bool):
            return a if cond else b
        return jnp.where(cond, a, b)

    weight_copy = pltpu.make_async_copy(w_ref, wbuf, wsem)
    weight_copy.start()
    blocks = tokens // QB
    here = meta_ref[blocks]

    def lay(order):
        at = 0
        for ref in order:
            kv_ref[at : at + ref.shape[0], :] = ref[...]
            at += ref.shape[0]

    if outputs == 2:

        @pl.when(here == 0)
        def _():
            lay((shards[1], shards[0], shards[2]))

        @pl.when(here != 0)
        def _():
            lay(shards)

    else:
        lay(shards)

    def prepare():
        for h in range(heads):
            q3[pl.ds(h, tokens, stride=heads), :] = q_ref[:, h * DH : (h + 1) * DH].astype(f32)
        second = kv_ref[W1 - W2 :, 2 * DH : 3 * DH].astype(f32)
        second = jnp.broadcast_to(second[:, None, :], (tokens + W2, heads, DH))
        k2x[...] = second.reshape(k2x.shape).astype(bf16)
        k1n[...] = kv_ref[W1:, :DH]
        rowid[...] = iota(rowid.shape, 0).astype(f32).astype(bf16)
        laneid[...] = iota(laneid.shape, 1).astype(f32).astype(bf16)
        bad[...] = jnp.zeros_like(bad)
        for k in range(tiles):
            own = kv_ref[W1 + k * LANES : W1 + (k + 1) * LANES, DH : 2 * DH]
            v1n[k, :DH] = own.astype(f32).T.astype(bf16)
            v1n[k, DH:] = jnp.ones((VR - DH, LANES), bf16)
        near = LANES + tokens
        v2t = kv_ref[W1 - LANES :, 3 * DH :].astype(f32).T
        v2t = jnp.concatenate([v2t, jnp.ones((VR - DH, near), f32)], axis=0).astype(bf16)
        first = LANES - W2
        for k in range((tokens + W2) // group):
            pick = iota((near, LANES), 0) == first + k * group + iota((near, LANES), 1) // heads
            v2x[k] = jnp.dot(v2t, pick.astype(f32).astype(bf16), preferred_element_type=f32)

    def reset(t, inv):
        kt = kv_ref[pl.ds(pl.multiple_of(W1 + t, PACK), PACK), :].astype(f32)[:1]
        window = kv_ref[:W1, : 2 * DH].astype(f32)
        ok = iota((W1, DH), 0) >= inv
        k1s[...] = jnp.where(ok, window[:, :DH], kt[:, :DH]).astype(bf16)
        values = jnp.where(ok, window[:, DH:], 0.0)
        for k in range(W1 // LANES):
            v1t[k, :DH] = values[k * LANES : (k + 1) * LANES].T.astype(bf16)
            live = k * LANES + iota((VR - DH, LANES), 1) >= inv
            v1t[k, DH:] = live.astype(f32).astype(bf16)
        k1n[...] = jnp.where(iota((tokens, DH), 0) < t, kt[:, :DH], k1n[...].astype(f32)).astype(bf16)
        for k in range(tiles):
            gone = k * LANES + iota((VR, LANES), 1) < t
            v1n[k] = jnp.where(gone, 0.0, v1n[k].astype(f32)).astype(bf16)

        @pl.when(inv == W1)
        def _():
            fill = jnp.broadcast_to(kt[:, 2 * DH : 3 * DH], (size, DH)).astype(bf16)
            for s in range(W2 // pack):
                k2x[t // pack + s] = fill
            for k in range(near_tiles):
                v2x[t // group + k] = jnp.zeros((VR, LANES), f32)

    def scores(g, u):
        t = g * group + u
        mark = t.astype(f32).astype(bf16)
        keys = [
            jnp.where(rowid[...] + (k * LANES) <= mark, k1n[k * LANES : (k + 1) * LANES], k1s[k * LANES : (k + 1) * LANES])
            for k in range(tiles)
        ]
        keys = jnp.concatenate(keys + [k1s[tokens:]], axis=0)
        query = q3[pl.ds(t * heads, heads), :]
        if heads < PACK:
            query = jnp.concatenate([query] * pack, axis=0)
        query = query.astype(bf16)
        base = g * (group // pack)
        for n in range(0, cols, wide):
            paired = []
            for s in range(n // size, (n + wide) // size):
                if s * pack >= group:
                    near_keys = k2x[base + s]
                elif pack == 1:
                    near_keys = k2x[base + either(s <= u, s + W2, s)]
                else:
                    token = s * pack + iota((size, DH), 0) // heads
                    after = k2x[base + s + W2 // pack].astype(f32)
                    near_keys = jnp.where(token <= u, after, k2x[base + s].astype(f32)).astype(bf16)
                paired.append(near_keys * query)
            yield lax.dot_general(
                keys,
                jnp.concatenate(paired, axis=0),
                (((1,), (1,)), ((), ())),
                preferred_element_type=f32,
            )

    def highest(logits, best=None):
        top = jnp.max(logits, axis=0, keepdims=True)
        for k in range(0, wide, LANES):
            some = top[:, k : k + LANES]
            best = some if best is None else jnp.maximum(best, some)
        return best

    def mix(g, u, n, logits, top):
        mark = (g * group + u).astype(f32).astype(bf16)
        values = [
            jnp.where(laneid[...] + (k * LANES) <= mark, v1n[k], v1t[k]) for k in range(tiles)
        ] + [v1t[k] for k in range(tiles, W1 // LANES)]
        tops = jnp.concatenate([top] * (wide // LANES), axis=1)
        product = None
        for k in range(0, W1, 2 * LANES):
            weights = jnp.exp2(logits[k : k + 2 * LANES] * scale - tops).astype(bf16)
            two = jnp.concatenate(values[k // LANES : k // LANES + 2], axis=1)
            some = jnp.dot(two, weights, preferred_element_type=f32)
            product = some if product is None else product + some
        total = None
        for c in range(0, wide, LANES):
            k = (n + c) // LANES
            near = v2x[g + k]
            if k == 0:
                near = jnp.where(iota((VR, LANES), 1) // heads <= u, v2x[g + near_tiles], near)
            some = product[:, c : c + LANES] * near
            total = some if total is None else total + some
        return total

    def keep(g, u, total, top):
        part[g * group + u] = total
        top2[g * group + u] = jnp.broadcast_to(top, (8, LANES))
        bad[...] = jnp.where(total[DH : DH + 8] < LIMIT, bad[...], 1.0)

    def finish(g):
        lane = iota((VR, LANES), 1)
        sums = []
        for u in range(group):
            top = top2[g * group + u]
            best = top
            shift = LANES // 2
            while shift >= heads:
                best = jnp.maximum(best, pltpu.roll(best, shift, 1))
                shift //= 2
            sums.append(part[g * group + u] * jnp.exp2(top - best)[:1])
        shift = heads
        while shift < LANES:
            low = lane % (2 * shift) < shift
            sums = [
                jnp.where(low, a, b) + pltpu.roll(jnp.where(low, b, a), shift, 1)
                for a, b in zip(sums[::2], sums[1::2])
            ]
            shift *= 2
        value = sums[0][:DH] * (1.0 / sums[0][DH : DH + 1])
        rows[pl.ds(pl.multiple_of(g * LANES, LANES), LANES), :] = value.T

    def run(exact):
        prepare()

        def block(b, _):
            inv = meta_ref[b]
            g0 = b * (QB // group)

            @pl.when((b == 0) | (inv == W1))
            def _():
                reset(b * QB, inv)

            def fast(s, _):
                g = g0 + s
                work = []
                for u in range(group):
                    work += [(u, n) for n in range(0, cols, wide)]
                source = {u: scores(g, u) for u in range(group)}
                top = total = None
                ahead = [next(source[u]) for u, n in work[:AHEAD]]
                for i, (u, n) in enumerate(work):
                    if i + AHEAD < len(work):
                        ahead.append(next(source[work[i + AHEAD][0]]))
                    logits = ahead.pop(0)
                    if n == 0:
                        top = highest(logits[:SAMPLE]) * scale
                        total = None
                    some = mix(g, u, n, logits, top)
                    total = some if total is None else total + some
                    if n + wide == cols:
                        keep(g, u, total, top)
                    if i == 0:
                        finish(jnp.maximum(g - 1, 0))
                return 0

            def slow(s, _):
                g, u = g0 + s // group, s % group
                best = None
                for logits in scores(g, u):
                    best = highest(logits, best)
                total = None
                for n, logits in zip(range(0, cols, wide), scores(g, u)):
                    some = mix(g, u, n, logits, best * scale)
                    total = some if total is None else total + some
                keep(g, u, total, best * scale)
                return 0

            if exact:
                return lax.fori_loop(0, QB, slow, 0)
            return lax.fori_loop(0, QB // group, fast, 0)

        lax.fori_loop(0, tokens // QB, block, 0)
        if exact:
            lax.fori_loop(0, tokens // group - 1, lambda g, _: finish(g) or 0, 0)
        finish(jnp.int32(tokens // group - 1))

    run(False)

    @pl.when(jnp.max(bad[...]) > 0)
    def _():
        run(True)

    attended = jnp.concatenate(
        [rows[pl.ds(h, tokens, stride=heads), :].astype(bf16) for h in range(heads)], axis=1
    )
    weight_copy.wait()
    width = out_refs[0].shape[1]
    step = 2 * LANES
    for k, out_ref in enumerate(out_refs):
        begin = 0 if outputs == 1 else jnp.where(here == k, width, 0)
        for n in range(0, width, step):
            some = wbuf[:, pl.ds(pl.multiple_of(begin + n, step), step)]
            out_ref[:, n : n + step] = jnp.dot(attended, some, preferred_element_type=f32)


def attended_and_projected(queries, shards, meta, weight, outputs):
    tokens, width = queries.shape
    heads = width // DH
    cols = W2 * heads
    size = max(heads, PACK)
    f32, bf16 = jnp.float32, jnp.bfloat16
    vmem = pl.BlockSpec(memory_space=pltpu.VMEM)
    return pl.pallas_call(
        functools.partial(attention_kernel, len(shards), outputs),
        out_shape=[jax.ShapeDtypeStruct((tokens, weight.shape[1] // outputs), f32)] * outputs,
        in_specs=[
            pl.BlockSpec(memory_space=pltpu.SMEM),
            vmem,
            pl.BlockSpec(memory_space=pl.ANY),
        ]
        + [vmem] * len(shards),
        out_specs=[vmem] * outputs,
        scratch_shapes=[
            pltpu.VMEM((W1 + tokens, 4 * DH), bf16),
            pltpu.VMEM(weight.shape, bf16),
            pltpu.SemaphoreType.DMA,
            pltpu.VMEM((tokens, DH), bf16),
            pltpu.VMEM((W1, DH), bf16),
            pltpu.VMEM((W1 // LANES, VR, LANES), bf16),
            pltpu.VMEM((tokens // LANES, VR, LANES), bf16),
            pltpu.VMEM(((tokens + W2) * heads // size, size, DH), bf16),
            pltpu.VMEM(((tokens + W2) * heads // LANES, VR, LANES), f32),
            pltpu.VMEM((LANES, DH), bf16),
            pltpu.VMEM((VR, LANES), bf16),
            pltpu.VMEM((tokens * heads, DH), f32),
            pltpu.VMEM((tokens, VR, LANES), f32),
            pltpu.VMEM((tokens, 8, LANES), f32),
            pltpu.VMEM((8, LANES), f32),
            pltpu.VMEM((tokens * heads, DH), f32),
        ],
        compiler_params=pltpu.CompilerParams(vmem_limit_bytes=40 * 2**20),
    )(meta, queries, weight, *shards)

HOPS = 3


def shifted(block, axis, distance):
    devices = range(lax.axis_size(axis))
    return lax.ppermute(block, axis, [(i - distance, i) for i in devices if i - distance in devices])


def swapped(block, axis, bits):
    return lax.ppermute(block, axis, [(i, i ^ bits) for i in range(lax.axis_size(axis))])


def collect_window(kv_rows, back):
    if lax.axis_size("head") != 2 or back != 4:
        return [shifted(kv_rows, "ctx", back - k) for k in range(back)] + [kv_rows]

    def taken(distances):
        devices = range(lax.axis_size("ctx"))
        route = [
            ((i - d) * 2 + h, i * 2 + h) for i in devices for h, d in enumerate(distances) if i >= d
        ]
        return lax.ppermute(kv_rows, ("ctx", "head"), route)

    held = jnp.concatenate([taken((2, 4)), taken((1, 3))], axis=0)
    return [held, swapped(held, "head", 1), kv_rows]


def body(queries, kv_rows, doc_start, destination, out_weight):
    position = lax.axis_index("ctx")
    tokens = queries.shape[0]
    blocks = tokens // QB
    group = HOPS + 1
    back = W1 // tokens
    shards = collect_window(kv_rows, back)
    first = position * blocks
    starts = lax.dynamic_slice_in_dim(doc_start, first, blocks, 0)
    own_rows = (first + jnp.arange(blocks, dtype=jnp.int32)) * QB
    inval = jnp.clip(starts - (own_rows - W1), 0, W1).astype(jnp.int32)
    place = position % group
    slots = group * blocks
    targets = lax.dynamic_slice_in_dim(destination, first - place * blocks, slots, 0)
    row = jnp.arange(group * tokens, dtype=jnp.int32)
    source = (place ^ (row // tokens)) * blocks + row % tokens // QB
    known = source[:, None] == jnp.arange(slots, dtype=jnp.int32)[None, :]
    target = jnp.sum(jnp.where(known, targets[None, :], 0), axis=1) * QB + row % QB
    pick = target[:, None] == (first * QB + jnp.arange(tokens, dtype=jnp.int32))[None, :]
    pick = pick.astype(jnp.bfloat16)
    here = lax.axis_index("head").astype(jnp.int32)
    meta = jnp.concatenate([inval, here[None]])
    outputs = 2 if len(shards) == 3 else 1
    partials = attended_and_projected(queries, shards, meta, out_weight, outputs)
    if outputs == 2:
        summed = partials[1] + swapped(partials[0], "head", 1)
    else:
        summed = lax.psum_scatter(partials[0], "head", scatter_dimension=1, tiled=True)
    projected = summed.astype(jnp.bfloat16)
    pieces = jnp.concatenate(
        [projected] + [swapped(projected, "ctx", r) for r in range(1, group)], axis=0
    )
    return lax.dot_general(
        pieces, pick, (((0,), (0,)), ((), ())), preferred_element_type=jnp.float32
    ).astype(jnp.bfloat16)


def solution(mesh):
    in_specs = (P("ctx", "head"), P("ctx", None), P(), P(), P("head", None))
    return jax.shard_map(
        body, mesh=mesh, in_specs=in_specs, out_specs=P("head", "ctx"), check_vma=False
    )
```

time: 91.8 us -> 189 us (2.06)
  Pallas kernels: 45.8 us -> 152 us
  starting transfers between devices: 21 us -> 12 us
  matrix products: 5.94 us -> 1.28 us
  local copies, waits for them, and re-layouts: 2.13 us -> 5.43 us
    pallas_call x1, Pallas kernels: 45.8 us -> 152 us  [attended_and_projected(): pl.pallas_call(functools.partial(attention_kernel, len(shards), outputs),...]
    ppermute x4 -> x2, starting transfers between devices: 15.2 us -> 8.27 us  [taken(): return lax.ppermute(kv_rows, ('ctx', 'head'), route)]
    dot_general x1 -> x0, matrix products: 4.67 us -> none  [body(): partial = jnp.dot(attended, out_weight, preferred_element_type=jnp.float32)]
    unnamed x8 -> x9, local copies, waits for them, and re-layouts: 1.08 us -> 5.34 us
    ppermute x4 -> x5, starting transfers between devices: 5.74 us -> 3.68 us  [swapped(): lax.ppermute(block, axis, [(i, i ^ bits) for i in range(lax.axis_size(axi...]
    ppermute x4 -> x5, waiting for transfers between devices: 13.6 us -> 12.9 us  [swapped(): lax.ppermute(block, axis, [(i, i ^ bits) for i in range(lax.axis_size(axi...]
  transfers between devices with their start and end apart: 8 -> 7, of which waited for: 5 -> 5; matrix products, arithmetic and copies ran while one was open for 1% -> 1% of each run, Pallas kernels for 0% -> 0%
where the time goes in v2:
time: 189 us; the launch traced here: 188 us
  Pallas kernels  152 us (80%)
  waiting for transfers between devices  16.7 us (9%)
  starting transfers between devices  12 us (6%)
  local copies, waits for them, and re-layouts  5.43 us (3%)
    pallas_call x1, Pallas kernels, attended_and_projected(): pl.pallas_call(functools.partial(attention_kernel, len(shards), outputs),...  152 us
    ppermute x5, waiting for transfers between devices, swapped(): lax.ppermute(block, axis, [(i, i ^ bits) for i in range(lax.axis_size(axi...  12.9 us
    ppermute x2, starting transfers between devices, taken(): return lax.ppermute(kv_rows, ('ctx', 'head'), route)  8.27 us
    unnamed x9, local copies, waits for them, and re-layouts  5.34 us
  transfers between devices with their start and end apart: 7, of which 5 were waited for; matrix products, arithmetic and copies ran while one was open for 1% of the time, Pallas kernels for 0%

profile of v2, /device:TPU:0, one launch (start us, length us, event | category | flops | bytes accessed | tf_op | source)
XLA Modules:
  0.0 188.2 jit_solution(2056665726668723911)
XLA Ops:
  0.0 4.9 %collective-permute-start = (bf16[128,512]{1,0:T(8,128)(2,1)}, bf16[128,512]{1,0:T(8,128)(2,1)S(1)}, u32[]{:S(2)}, u32[]{:S(2)}) collective-permute-start(bf16[128,512]{1,0:T(8,128)(2,1)} %refs_2_.1), channel_id=1, source_target_pairs={{0,4},{2,6},{4,8},{1,9},{6,10},{3,11},{8,12},{5,13},{10,14},{7,15}... | collective-permute-start | bytes 393224 | tf_op jit(solution)/shard_map/ppermute | solution.py:338
  4.9 3.4 %collective-permute-start.1 = (bf16[128,512]{1,0:T(8,128)(2,1)}, bf16[128,512]{1,0:T(8,128)(2,1)S(1)}, u32[]{:S(2)}, u32[]{:S(2)}) collective-permute-start(bf16[128,512]{1,0:T(8,128)(2,1)} %refs_2_.1), channel_id=1, source_target_pairs={{0,2},{2,4},{4,6},{1,7},{6,8},{3,9},{8,10},{5,11},{10,12},{7,13},{... | collective-permute-start | bytes 393224 | tf_op jit(solution)/shard_map/ppermute | solution.py:338
  8.3 0.0 collective-permute-done
  8.3 3.7 %collective-permute-done.1 = bf16[128,512]{1,0:T(8,128)(2,1)S(1)} collective-permute-done((bf16[128,512]{1,0:T(8,128)(2,1)}, bf16[128,512]{1,0:T(8,128)(2,1)S(1)}, u32[]{:S(2)}, u32[]{:S(2)}) %collective-permute-start.1) | collective-permute-done | bytes 131104 | tf_op jit(solution)/shard_map/ppermute | solution.py:338
  12.1 0.1 collective-permute-start.2
  12.2 0.7 subtract_clamp_fusion
  12.9 0.1 pad_add_fusion.meta_ref
  13.0 0.7 collective-permute-done.2.refs_1_
  13.7 3.4 %copy-done = bf16[2048,2048]{1,0:T(8,128)(2,1)S(1)} copy-done((bf16[2048,2048]{1,0:T(8,128)(2,1)S(1)}, bf16[2048,2048]{1,0:T(8,128)(2,1)}, u32[]{:S(2)}) %copy-start) | copy-done | bytes 8388632
  17.1 1.0 copy-done.1
  18.1 0.9 copy-done.2
  19.0 151.7 %shard_map.55 = (f32[128,1024]{1,0:T(8,128)S(1)}, f32[128,1024]{1,0:T(8,128)S(1)}) custom-call(s32[5]{0:T(128)S(1)} %pad_add_fusion.meta_ref, bf16[128,2048]{1,0:T(8,128)(2,1)S(1)} %copy-done.1, bf16[2048,2048]{1,0:T(8,128)(2,1)S(1)} %copy-done, bf16[256,512]{1,0:T(8,128)(2,1)S(1)} %constant_dynamic-update-slice_fusion.refs_0_, ...), custom_call_target="tpu_custom_call" | custom-call | tf_op jit(solution)/shard_map/pallas_call | solution.py:286
  170.7 0.1 collective-permute-start.3
  170.8 0.1 dynamic_slice.7
  170.9 0.1 select_reduce_fusion
  171.0 1.7 collective-permute-done.3
  172.7 0.1 add_convert_fusion
  172.8 0.1 collective-permute-start.6
  172.8 0.1 collective-permute-start.5
  172.9 3.4 %collective-permute-start.4 = (bf16[128,1024]{1,0:T(8,128)(2,1)S(1)}, bf16[128,1024]{1,0:T(8,128)(2,1)S(1)}, u32[]{:S(2)}, u32[]{:S(2)}) collective-permute-start(bf16[128,1024]{1,0:T(8,128)(2,1)S(1)} %add_convert_fusion), channel_id=1, source_target_pairs={{0,2},{2,0},{4,6},{6,4},{8,10},{10,8},{12,14},{14,12},{16,18},{18,... | collective-permute-start | bytes 786440 | tf_op jit(solution)/shard_map/ppermute | solution.py:326
  176.3 6.6 %collective-permute-done.6 = bf16[128,1024]{1,0:T(8,128)(2,1)S(1)} collective-permute-done((bf16[128,1024]{1,0:T(8,128)(2,1)S(1)}, bf16[128,1024]{1,0:T(8,128)(2,1)S(1)}, u32[]{:S(2)}, u32[]{:S(2)}) %collective-permute-start.6) | collective-permute-done | bytes 262176 | tf_op jit(solution)/shard_map/ppermute | solution.py:326
  182.9 3.9 %collective-permute-done.5 = bf16[128,1024]{1,0:T(8,128)(2,1)S(1)} collective-permute-done((bf16[128,1024]{1,0:T(8,128)(2,1)S(1)}, bf16[128,1024]{1,0:T(8,128)(2,1)S(1)}, u32[]{:S(2)}, u32[]{:S(2)}) %collective-permute-start.5) | collective-permute-done | bytes 262176 | tf_op jit(solution)/shard_map/ppermute | solution.py:326
  186.9 0.0 collective-permute-done.4
  186.9 1.3 convolution_convert_fusion
  (10 shorter events, 0.0 us)
Async XLA Ops:
  0.0 8.3 %collective-permute-start = (bf16[128,512]{1,0:T(8,128)(2,1)}, bf16[128,512]{1,0:T(8,128)(2,1)S(1)}, u32[]{:S(2)}, u32[]{:S(2)}) collective-permute-start(bf16[128,512]{1,0:T(8,128)(2,1)} %refs_2_.1), channel_id=1, source_target_pairs={{0,4},{2,6},{4,8},{1,9},{6,10},{3,11},{8,12},{5,13},{10,14},{7,15}... | collective-permute-start | bytes 393224 | tf_op jit(solution)/shard_map/ppermute | solution.py:338
  4.9 7.2 %collective-permute-start.1 = (bf16[128,512]{1,0:T(8,128)(2,1)}, bf16[128,512]{1,0:T(8,128)(2,1)S(1)}, u32[]{:S(2)}, u32[]{:S(2)}) collective-permute-start(bf16[128,512]{1,0:T(8,128)(2,1)} %refs_2_.1), channel_id=1, source_target_pairs={{0,2},{2,4},{4,6},{1,7},{6,8},{3,9},{8,10},{5,11},{10,12},{7,13},{... | collective-permute-start | bytes 393224 | tf_op jit(solution)/shard_map/ppermute | solution.py:338
  12.1 1.6 collective-permute-start.2
  13.7 3.4 %copy-start = (bf16[2048,2048]{1,0:T(8,128)(2,1)S(1)}, bf16[2048,2048]{1,0:T(8,128)(2,1)}, u32[]{:S(2)}) copy-start(bf16[2048,2048]{1,0:T(8,128)(2,1)} %w_ref.1) | copy-start | bytes 25165828
  17.1 1.0 copy-start.1
  18.1 0.9 copy-start.2
  19.0 151.8 %copy-start.3 = (s32[64]{0:T(128)S(1)}, s32[64]{0:T(128)}, u32[]{:S(2)}) copy-start(s32[64]{0:T(128)} %param.8) | copy-start | bytes 772
  170.7 2.0 %collective-permute-start.3 = (f32[128,1024]{1,0:T(8,128)S(1)}, f32[128,1024]{1,0:T(8,128)S(1)}, u32[]{:S(2)}, u32[]{:S(2)}) collective-permute-start(f32[128,1024]{1,0:T(8,128)S(1)} %get-tuple-element.8), channel_id=1, source_target_pairs={{0,1},{1,0},{2,3},{3,2},{4,5},{5,4},{6,7},{7,6},{8,9},{9,8},{10,11... | collective-permute-start | bytes 1572872 | tf_op jit(solution)/shard_map/ppermute | solution.py:326
  172.8 10.2 %collective-permute-start.6 = (bf16[128,1024]{1,0:T(8,128)(2,1)S(1)}, bf16[128,1024]{1,0:T(8,128)(2,1)S(1)}, u32[]{:S(2)}, u32[]{:S(2)}) collective-permute-start(bf16[128,1024]{1,0:T(8,128)(2,1)S(1)} %add_convert_fusion), channel_id=1, source_target_pairs={{0,6},{2,4},{4,2},{6,0},{8,14},{10,12},{12,10},{14,8},{16,22},{18,... | collective-permute-start | bytes 786440 | tf_op jit(solution)/shard_map/ppermute | solution.py:326
  172.8 14.0 %collective-permute-start.5 = (bf16[128,1024]{1,0:T(8,128)(2,1)S(1)}, bf16[128,1024]{1,0:T(8,128)(2,1)S(1)}, u32[]{:S(2)}, u32[]{:S(2)}) collective-permute-start(bf16[128,1024]{1,0:T(8,128)(2,1)S(1)} %add_convert_fusion), channel_id=1, source_target_pairs={{0,4},{2,6},{4,0},{6,2},{8,12},{10,14},{12,8},{14,10},{16,20},{18,... | collective-permute-start | bytes 786440 | tf_op jit(solution)/shard_map/ppermute | solution.py:326
  172.9 14.0 %collective-permute-start.4 = (bf16[128,1024]{1,0:T(8,128)(2,1)S(1)}, bf16[128,1024]{1,0:T(8,128)(2,1)S(1)}, u32[]{:S(2)}, u32[]{:S(2)}) collective-permute-start(bf16[128,1024]{1,0:T(8,128)(2,1)S(1)} %add_convert_fusion), channel_id=1, source_target_pairs={{0,2},{2,0},{4,6},{6,4},{8,10},{10,8},{12,14},{14,12},{16,18},{18,... | collective-permute-start | bytes 786440 | tf_op jit(solution)/shard_map/ppermute | solution.py:326

commit v3 on v2

--- a/solution.py
+++ b/solution.py
@@ -21,12 +21,46 @@
 LOG2E = 1.4426950408889634
 
 
-def attention_kernel(pairs, outputs, meta_ref, q_ref, w_ref, *refs):
+def iota(shape, dim):
+    return lax.broadcasted_iota(jnp.int32, shape, dim)
+
+
+def spread(columns, first, heads):
+    pick = iota((columns.shape[1], LANES), 0) == first + iota((columns.shape[1], LANES), 1) // heads
+    pick = pick.astype(jnp.float32).astype(jnp.bfloat16)
+    return jnp.dot(columns, pick, preferred_element_type=jnp.float32)
+
+
+def with_ones(values):
+    return jnp.concatenate(
+        [values.astype(jnp.float32).T, jnp.ones((VR - DH, LANES), jnp.float32)], axis=0
+    ).astype(jnp.bfloat16)
+
+
+def own_kernel(q_ref, kv_ref, q3, k1o, v1o, k2o, v2o):
+    f32, bf16 = jnp.float32, jnp.bfloat16
+    tokens = q_ref.shape[0]
+    heads = q_ref.shape[1] // DH
+    group = LANES // heads
+    k1o[...] = kv_ref[:, :DH]
+    second = kv_ref[:, 2 * DH : 3 * DH].astype(f32)
+    second = jnp.broadcast_to(second[:, None, :], (tokens, heads, DH))
+    k2o[...] = second.reshape(k2o.shape).astype(bf16)
+    for k in range(tokens // LANES):
+        v1o[k] = with_ones(kv_ref[k * LANES : (k + 1) * LANES, DH : 2 * DH])
+        columns = with_ones(kv_ref[k * LANES : (k + 1) * LANES, 3 * DH :])
+        for c in range(heads):
+            v2o[k * heads + c] = spread(columns, c * group, heads)
+    for h in range(heads):
+        q3[pl.ds(h, tokens, stride=heads), :] = q_ref[:, h * DH : (h + 1) * DH].astype(f32)
+
+
+def attention_kernel(pairs, outputs, meta_ref, q3, k1o, v1o, k2o, v2o, w_ref, *refs):
     shards, refs = refs[:pairs], refs[pairs:]
     out_refs, refs = refs[:outputs], refs[outputs:]
-    kv_ref, wbuf, wsem, k1n, k1s, v1t, v1n, k2x, v2x, rowid, laneid, q3, part, top2, bad, rows = refs
-    tokens = q_ref.shape[0]
-    heads = q_ref.shape[1] // DH
+    kv_ref, wbuf, wsem, k1n, k1s, v1t, v1n, k2x, v2x, rowid, laneid, part, top2, bad, rows = refs
+    tokens = k1o.shape[0]
+    heads = q3.shape[0] // tokens
     cols = W2 * heads
     group = LANES // heads
     tiles = tokens // LANES
@@ -37,9 +71,6 @@
     scale = LOG2E / np.sqrt(DH)
     f32, bf16 = jnp.float32, jnp.bfloat16
 
-    def iota(shape, dim):
-        return lax.broadcasted_iota(jnp.int32, shape, dim)
-
     def either(cond, a, b):
         if isinstance(cond, bool):
             return a if cond else b
@@ -60,7 +91,7 @@
 
         @pl.when(here == 0)
         def _():
-            lay((shards[1], shards[0], shards[2]))
+            lay(shards[::-1])
 
         @pl.when(here != 0)
         def _():
@@ -70,45 +101,38 @@
         lay(shards)
 
     def prepare():
-        for h in range(heads):
-            q3[pl.ds(h, tokens, stride=heads), :] = q_ref[:, h * DH : (h + 1) * DH].astype(f32)
-        second = kv_ref[W1 - W2 :, 2 * DH : 3 * DH].astype(f32)
-        second = jnp.broadcast_to(second[:, None, :], (tokens + W2, heads, DH))
-        k2x[...] = second.reshape(k2x.shape).astype(bf16)
-        k1n[...] = kv_ref[W1:, :DH]
         rowid[...] = iota(rowid.shape, 0).astype(f32).astype(bf16)
         laneid[...] = iota(laneid.shape, 1).astype(f32).astype(bf16)
         bad[...] = jnp.zeros_like(bad)
-        for k in range(tiles):
-            own = kv_ref[W1 + k * LANES : W1 + (k + 1) * LANES, DH : 2 * DH]
-            v1n[k, :DH] = own.astype(f32).T.astype(bf16)
-            v1n[k, DH:] = jnp.ones((VR - DH, LANES), bf16)
-        near = LANES + tokens
-        v2t = kv_ref[W1 - LANES :, 3 * DH :].astype(f32).T
-        v2t = jnp.concatenate([v2t, jnp.ones((VR - DH, near), f32)], axis=0).astype(bf16)
-        first = LANES - W2
-        for k in range((tokens + W2) // group):
-            pick = iota((near, LANES), 0) == first + k * group + iota((near, LANES), 1) // heads
-            v2x[k] = jnp.dot(v2t, pick.astype(f32).astype(bf16), preferred_element_type=f32)
+        k1n[...] = k1o[...]
+        v1n[...] = v1o[...]
+        second = kv_ref[W1 - W2 :, 2 * DH : 3 * DH].astype(f32)
+        second = jnp.broadcast_to(second[:, None, :], (W2, heads, DH))
+        k2x[: W2 // pack] = second.reshape(W2 // pack, size, DH).astype(bf16)
+        k2x[W2 // pack :] = k2o[...]
+        columns = with_ones(kv_ref[W1 - LANES :, 3 * DH :])
+        for k in range(near_tiles):
+            v2x[k] = spread(columns, LANES - W2 + k * group, heads)
+        v2x[near_tiles:] = v2o[...]
 
     def reset(t, inv):
-        kt = kv_ref[pl.ds(pl.multiple_of(W1 + t, PACK), PACK), :].astype(f32)[:1]
-        window = kv_ref[:W1, : 2 * DH].astype(f32)
+        kt = k1o[pl.ds(pl.multiple_of(t, PACK), PACK), :].astype(f32)[:1]
+        window = kv_ref[:, : 2 * DH].astype(f32)
         ok = iota((W1, DH), 0) >= inv
-        k1s[...] = jnp.where(ok, window[:, :DH], kt[:, :DH]).astype(bf16)
+        k1s[...] = jnp.where(ok, window[:, :DH], kt).astype(bf16)
         values = jnp.where(ok, window[:, DH:], 0.0)
         for k in range(W1 // LANES):
             v1t[k, :DH] = values[k * LANES : (k + 1) * LANES].T.astype(bf16)
             live = k * LANES + iota((VR - DH, LANES), 1) >= inv
             v1t[k, DH:] = live.astype(f32).astype(bf16)
-        k1n[...] = jnp.where(iota((tokens, DH), 0) < t, kt[:, :DH], k1n[...].astype(f32)).astype(bf16)
+        k1n[...] = jnp.where(iota((tokens, DH), 0) < t, kt, k1n[...].astype(f32)).astype(bf16)
         for k in range(tiles):
             gone = k * LANES + iota((VR, LANES), 1) < t
             v1n[k] = jnp.where(gone, 0.0, v1n[k].astype(f32)).astype(bf16)
 
         @pl.when(inv == W1)
         def _():
-            fill = jnp.broadcast_to(kt[:, 2 * DH : 3 * DH], (size, DH)).astype(bf16)
+            fill = jnp.broadcast_to(k2x[(t + W2) // pack].astype(f32)[:1], (size, DH)).astype(bf16)
             for s in range(W2 // pack):
                 k2x[t // pack + s] = fill
             for k in range(near_tiles):
@@ -276,25 +300,43 @@
             out_ref[:, n : n + step] = jnp.dot(attended, some, preferred_element_type=f32)
 
 
-def attended_and_projected(queries, shards, meta, weight, outputs):
+VMEM = pl.BlockSpec(memory_space=pltpu.VMEM)
+HBM = pl.BlockSpec(memory_space=pltpu.HBM)
+
+
+def own_layouts(queries, kv_rows):
     tokens, width = queries.shape
     heads = width // DH
-    cols = W2 * heads
     size = max(heads, PACK)
     f32, bf16 = jnp.float32, jnp.bfloat16
-    vmem = pl.BlockSpec(memory_space=pltpu.VMEM)
+    return pl.pallas_call(
+        own_kernel,
+        out_shape=[
+            jax.ShapeDtypeStruct((tokens * heads, DH), f32),
+            jax.ShapeDtypeStruct((tokens, DH), bf16),
+            jax.ShapeDtypeStruct((tokens // LANES, VR, LANES), bf16),
+            jax.ShapeDtypeStruct((tokens * heads // size, size, DH), bf16),
+            jax.ShapeDtypeStruct((tokens * heads // LANES, VR, LANES), f32),
+        ],
+        in_specs=[VMEM] * 2,
+        out_specs=[VMEM] * 5,
+        compiler_params=pltpu.CompilerParams(vmem_limit_bytes=16 * 2**20),
+        cost_estimate=pl.CostEstimate(flops=10**9, bytes_accessed=4 * 2**20, transcendentals=0),
+    )(queries, kv_rows)
+
+
+def attended_and_projected(own, shards, meta, weight, outputs):
+    heads = own[0].shape[0] // own[1].shape[0]
+    tokens = own[1].shape[0]
+    size = max(heads, PACK)
+    f32, bf16 = jnp.float32, jnp.bfloat16
     return pl.pallas_call(
         functools.partial(attention_kernel, len(shards), outputs),
         out_shape=[jax.ShapeDtypeStruct((tokens, weight.shape[1] // outputs), f32)] * outputs,
-        in_specs=[
-            pl.BlockSpec(memory_space=pltpu.SMEM),
-            vmem,
-            pl.BlockSpec(memory_space=pl.ANY),
-        ]
-        + [vmem] * len(shards),
-        out_specs=[vmem] * outputs,
+        in_specs=[pl.BlockSpec(memory_space=pltpu.SMEM)] + [VMEM] * 5 + [HBM] + [VMEM] * len(shards),
+        out_specs=[VMEM] * outputs,
         scratch_shapes=[
-            pltpu.VMEM((W1 + tokens, 4 * DH), bf16),
+            pltpu.VMEM((W1, 4 * DH), bf16),
             pltpu.VMEM(weight.shape, bf16),
             pltpu.SemaphoreType.DMA,
             pltpu.VMEM((tokens, DH), bf16),
@@ -305,14 +347,13 @@
             pltpu.VMEM(((tokens + W2) * heads // LANES, VR, LANES), f32),
             pltpu.VMEM((LANES, DH), bf16),
             pltpu.VMEM((VR, LANES), bf16),
-            pltpu.VMEM((tokens * heads, DH), f32),
             pltpu.VMEM((tokens, VR, LANES), f32),
             pltpu.VMEM((tokens, 8, LANES), f32),
             pltpu.VMEM((8, LANES), f32),
             pltpu.VMEM((tokens * heads, DH), f32),
         ],
-        compiler_params=pltpu.CompilerParams(vmem_limit_bytes=40 * 2**20),
-    )(meta, queries, weight, *shards)
+        compiler_params=pltpu.CompilerParams(vmem_limit_bytes=46 * 2**20),
+    )(meta, *own, weight, *shards)
 
 HOPS = 3
 
@@ -326,9 +367,9 @@
     return lax.ppermute(block, axis, [(i, i ^ bits) for i in range(lax.axis_size(axis))])
 
 
-def collect_window(kv_rows, back):
+def collect_window(kv_rows, back, own):
     if lax.axis_size("head") != 2 or back != 4:
-        return [shifted(kv_rows, "ctx", back - k) for k in range(back)] + [kv_rows]
+        return [shifted(kv_rows, "ctx", back - k) for k in range(back)], own
 
     def taken(distances):
         devices = range(lax.axis_size("ctx"))
@@ -337,8 +378,9 @@
         ]
         return lax.ppermute(kv_rows, ("ctx", "head"), route)
 
-    held = jnp.concatenate([taken((2, 4)), taken((1, 3))], axis=0)
-    return [held, swapped(held, "head", 1), kv_rows]
+    parts, own = lax.optimization_barrier(([taken((2, 4)), taken((1, 3))], own))
+    held = jnp.concatenate(parts, axis=0)
+    return [held, swapped(held, "head", 1)], own
 
 
 def body(queries, kv_rows, doc_start, destination, out_weight):
@@ -347,7 +389,7 @@
     blocks = tokens // QB
     group = HOPS + 1
     back = W1 // tokens
-    shards = collect_window(kv_rows, back)
+    shards, own = collect_window(kv_rows, back, own_layouts(queries, kv_rows))
     first = position * blocks
     starts = lax.dynamic_slice_in_dim(doc_start, first, blocks, 0)
     own_rows = (first + jnp.arange(blocks, dtype=jnp.int32)) * QB
@@ -363,8 +405,8 @@
     pick = pick.astype(jnp.bfloat16)
     here = lax.axis_index("head").astype(jnp.int32)
     meta = jnp.concatenate([inval, here[None]])
-    outputs = 2 if len(shards) == 3 else 1
-    partials = attended_and_projected(queries, shards, meta, out_weight, outputs)
+    outputs = 2 if len(shards) == 2 else 1
+    partials = attended_and_projected(own, shards, meta, out_weight, outputs)
     if outputs == 2:
         summed = partials[1] + swapped(partials[0], "head", 1)
     else:

time: 189 us -> 186 us (0.984)
  Pallas kernels: 152 us -> 40.8 us
  starting transfers between devices: 12 us -> 123 us
  waiting for transfers between devices: 16.7 us -> 14.8 us
    pallas_call x1, Pallas kernels: 152 us -> 39.8 us  [attended_and_projected(): pl.pallas_call(functools.partial(attention_kernel, len(shards), outputs),...]
    ppermute x5, starting transfers between devices: 3.68 us -> 114 us  [swapped(): lax.ppermute(block, axis, [(i, i ^ bits) for i in range(lax.axis_size(axi...]
    ppermute x2, waiting for transfers between devices: 3.75 us -> 0.01 us  [taken(): return lax.ppermute(kv_rows, ('ctx', 'head'), route)]
    unnamed x9 -> x21, local copies, waits for them, and re-layouts: 5.34 us -> 6.34 us
  transfers between devices with their start and end apart: 7 -> 7, of which waited for: 5 -> 4; matrix products, arithmetic and copies ran while one was open for 1% -> 0% of each run, Pallas kernels for 0% -> 1%
where the time goes in v3:
time: 186 us
  starting transfers between devices  123 us (66%)
  Pallas kernels  40.8 us (22%)
  waiting for transfers between devices  14.8 us (8%)
  local copies, waits for them, and re-layouts  6.42 us (3%)
    ppermute x5, starting transfers between devices, swapped(): lax.ppermute(block, axis, [(i, i ^ bits) for i in range(lax.axis_size(axi...  114 us
    pallas_call x1, Pallas kernels, attended_and_projected(): pl.pallas_call(functools.partial(attention_kernel, len(shards), outputs),...  39.8 us
    ppermute x5, waiting for transfers between devices, swapped(): lax.ppermute(block, axis, [(i, i ^ bits) for i in range(lax.axis_size(axi...  14.8 us
    ppermute x2, starting transfers between devices, taken(): return lax.ppermute(kv_rows, ('ctx', 'head'), route)  8.27 us
    unnamed x21, local copies, waits for them, and re-layouts  6.34 us
  transfers between devices with their start and end apart: 7, of which 4 were waited for; matrix products, arithmetic and copies ran while one was open for 0% of the time, Pallas kernels for 1%

profile of v3, /device:TPU:0, one launch (start us, length us, event | category | flops | bytes accessed | tf_op | source)
XLA Modules:
  0.0 186.2 jit_solution(7021413927736855247)
XLA Ops:
  0.0 4.9 %collective-permute-start = (bf16[128,512]{1,0:T(8,128)(2,1)}, bf16[128,512]{1,0:T(8,128)(2,1)S(1)}, u32[]{:S(2)}, u32[]{:S(2)}) collective-permute-start(bf16[128,512]{1,0:T(8,128)(2,1)} %kv_ref.1), channel_id=1, source_target_pairs={{0,4},{2,6},{4,8},{1,9},{6,10},{3,11},{8,12},{5,13},{10,14},{7,15}... | collective-permute-start | bytes 393224 | tf_op jit(solution)/shard_map/ppermute | solution.py:379
  4.9 3.4 %collective-permute-start.1 = (bf16[128,512]{1,0:T(8,128)(2,1)}, bf16[128,512]{1,0:T(8,128)(2,1)S(1)}, u32[]{:S(2)}, u32[]{:S(2)}) collective-permute-start(bf16[128,512]{1,0:T(8,128)(2,1)} %kv_ref.1), channel_id=1, source_target_pairs={{0,2},{2,4},{4,6},{1,7},{6,8},{3,9},{8,10},{5,11},{10,12},{7,13},{... | collective-permute-start | bytes 393224 | tf_op jit(solution)/shard_map/ppermute | solution.py:379
  8.3 1.0 copy-done.6
  9.3 0.9 copy-done.7
  10.2 1.0 shard_map.55
  11.2 0.6 copy-done.2
  11.8 0.6 copy-done.4
  12.5 0.4 collective-permute-start.2
  12.8 0.1 subtract_clamp_fusion
  13.0 1.1 collective-permute-done.2.refs_1_
  14.1 0.7 copy-done
  14.8 0.9 copy-done.1
  15.7 0.8 copy-done.3
  16.5 0.8 copy-done.5
  17.3 39.8 %shard_map.56 = (f32[128,1024]{1,0:T(8,128)}, f32[128,1024]{1,0:T(8,128)S(1)}) custom-call(s32[5]{0:T(128)S(1)} %pad_add_fusion.meta_ref, f32[2048,128]{1,0:T(8,128)S(1)} %get-tuple-element.24.q3, bf16[128,128]{1,0:T(8,128)(2,1)S(1)} %copy-done.5, bf16[1,144,128]{2,1,0:T(8,128)(2,1)S(1)} %copy-done.3, bf16[128,16,128]{2,1,0:T(8,128)(2,1)S(1)} %get-tuple-element.27.k2o, ...), custom_call_target="tpu_custom_call" | custom-call | tf_op jit(solution)/shard_map/pallas_call | solution.py:333
  57.1 110.3 %collective-permute-start.3 = (f32[128,1024]{1,0:T(8,128)}, f32[128,1024]{1,0:T(8,128)S(1)}, u32[]{:S(2)}, u32[]{:S(2)}) collective-permute-start(f32[128,1024]{1,0:T(8,128)} %get-tuple-element.32), channel_id=1, source_target_pairs={{0,1},{1,0},{2,3},{3,2},{4,5},{5,4},{6,7},{7,6},{8,9},{9,8},{10,11... | collective-permute-start | bytes 1572872 | tf_op jit(solution)/shard_map/ppermute | solution.py:367
  167.5 0.1 select_reduce_fusion
  167.6 1.6 collective-permute-done.3
  169.2 2.1 %collective-permute-start.4 = (bf16[128,1024]{1,0:T(8,128)(2,1)S(1)}, bf16[128,1024]{1,0:T(8,128)(2,1)S(1)}, u32[]{:S(2)}, u32[]{:S(2)}) collective-permute-start(bf16[128,1024]{1,0:T(8,128)(2,1)S(1)} %add_convert_fusion), channel_id=1, source_target_pairs={{0,2},{2,0},{4,6},{6,4},{8,10},{10,8},{12,14},{14,12},{16,18},{18,... | collective-permute-start | bytes 786440 | tf_op jit(solution)/shard_map/ppermute | solution.py:367
  171.3 1.3 collective-permute-start.5
  172.6 0.2 collective-permute-start.6
  172.8 5.6 %collective-permute-done.4 = bf16[128,1024]{1,0:T(8,128)(2,1)S(1)} collective-permute-done((bf16[128,1024]{1,0:T(8,128)(2,1)S(1)}, bf16[128,1024]{1,0:T(8,128)(2,1)S(1)}, u32[]{:S(2)}, u32[]{:S(2)}) %collective-permute-start.4) | collective-permute-done | bytes 262176 | tf_op jit(solution)/shard_map/ppermute | solution.py:367
  178.4 6.6 %collective-permute-done.5 = bf16[128,1024]{1,0:T(8,128)(2,1)S(1)} collective-permute-done((bf16[128,1024]{1,0:T(8,128)(2,1)S(1)}, bf16[128,1024]{1,0:T(8,128)(2,1)S(1)}, u32[]{:S(2)}, u32[]{:S(2)}) %collective-permute-start.5) | collective-permute-done | bytes 262176 | tf_op jit(solution)/shard_map/ppermute | solution.py:367
  185.0 1.3 convolution_convert_fusion
  (23 shorter events, 0.3 us)
Async XLA Ops:
  0.0 12.5 %collective-permute-start = (bf16[128,512]{1,0:T(8,128)(2,1)}, bf16[128,512]{1,0:T(8,128)(2,1)S(1)}, u32[]{:S(2)}, u32[]{:S(2)}) collective-permute-start(bf16[128,512]{1,0:T(8,128)(2,1)} %kv_ref.1), channel_id=1, source_target_pairs={{0,4},{2,6},{4,8},{1,9},{6,10},{3,11},{8,12},{5,13},{10,14},{7,15}... | collective-permute-start | bytes 393224 | tf_op jit(solution)/shard_map/ppermute | solution.py:379
  4.9 7.6 %collective-permute-start.1 = (bf16[128,512]{1,0:T(8,128)(2,1)}, bf16[128,512]{1,0:T(8,128)(2,1)S(1)}, u32[]{:S(2)}, u32[]{:S(2)}) collective-permute-start(bf16[128,512]{1,0:T(8,128)(2,1)} %kv_ref.1), channel_id=1, source_target_pairs={{0,2},{2,4},{4,6},{1,7},{6,8},{3,9},{8,10},{5,11},{10,12},{7,13},{... | collective-permute-start | bytes 393224 | tf_op jit(solution)/shard_map/ppermute | solution.py:379
  8.3 1.0 copy-start.6
  9.3 0.9 copy-start.7
  10.2 2.6 %copy-start.8 = (s32[64]{0:T(128)S(1)}, s32[64]{0:T(128)}, u32[]{:S(2)}) copy-start(s32[64]{0:T(128)} %param.7) | copy-start | bytes 772
  11.2 0.6 copy-start.2
  11.8 0.6 copy-start.4
  12.5 1.6 collective-permute-start.2
  14.1 0.7 copy-start
  14.8 0.9 copy-start.1
  15.7 0.8 copy-start.3
  16.5 0.8 copy-start.5
  17.3 150.1 %copy-start.9 = (s32[64]{0:T(128)S(1)}, s32[64]{0:T(128)}, u32[]{:S(2)}) copy-start(s32[64]{0:T(128)} %param.8) | copy-start | bytes 772
  57.1 112.0 %collective-permute-start.3 = (f32[128,1024]{1,0:T(8,128)}, f32[128,1024]{1,0:T(8,128)S(1)}, u32[]{:S(2)}, u32[]{:S(2)}) collective-permute-start(f32[128,1024]{1,0:T(8,128)} %get-tuple-element.32), channel_id=1, source_target_pairs={{0,1},{1,0},{2,3},{3,2},{4,5},{5,4},{6,7},{7,6},{8,9},{9,8},{10,11... | collective-permute-start | bytes 1572872 | tf_op jit(solution)/shard_map/ppermute | solution.py:367
  169.2 9.2 %collective-permute-start.4 = (bf16[128,1024]{1,0:T(8,128)(2,1)S(1)}, bf16[128,1024]{1,0:T(8,128)(2,1)S(1)}, u32[]{:S(2)}, u32[]{:S(2)}) collective-permute-start(bf16[128,1024]{1,0:T(8,128)(2,1)S(1)} %add_convert_fusion), channel_id=1, source_target_pairs={{0,2},{2,0},{4,6},{6,4},{8,10},{10,8},{12,14},{14,12},{16,18},{18,... | collective-permute-start | bytes 786440 | tf_op jit(solution)/shard_map/ppermute | solution.py:367
  171.3 13.7 %collective-permute-start.5 = (bf16[128,1024]{1,0:T(8,128)(2,1)S(1)}, bf16[128,1024]{1,0:T(8,128)(2,1)S(1)}, u32[]{:S(2)}, u32[]{:S(2)}) collective-permute-start(bf16[128,1024]{1,0:T(8,128)(2,1)S(1)} %add_convert_fusion), channel_id=1, source_target_pairs={{0,4},{2,6},{4,0},{6,2},{8,12},{10,14},{12,8},{14,10},{16,20},{18,... | collective-permute-start | bytes 786440 | tf_op jit(solution)/shard_map/ppermute | solution.py:367
  172.6 12.3 %collective-permute-start.6 = (bf16[128,1024]{1,0:T(8,128)(2,1)S(1)}, bf16[128,1024]{1,0:T(8,128)(2,1)S(1)}, u32[]{:S(2)}, u32[]{:S(2)}) collective-permute-start(bf16[128,1024]{1,0:T(8,128)(2,1)S(1)} %add_convert_fusion), channel_id=1, source_target_pairs={{0,6},{2,4},{4,2},{6,0},{8,14},{10,12},{12,10},{14,8},{16,22},{18,... | collective-permute-start | bytes 786440 | tf_op jit(solution)/shard_map/ppermute | solution.py:367

commit v4 on v3

--- a/solution.py
+++ b/solution.py
@@ -352,7 +352,7 @@
             pltpu.VMEM((8, LANES), f32),
             pltpu.VMEM((tokens * heads, DH), f32),
         ],
-        compiler_params=pltpu.CompilerParams(vmem_limit_bytes=46 * 2**20),
+        compiler_params=pltpu.CompilerParams(vmem_limit_bytes=43 * 2**20),
     )(meta, *own, weight, *shards)
 
 HOPS = 3
@@ -381,6 +381,93 @@
     parts, own = lax.optimization_barrier(([taken((2, 4)), taken((1, 3))], own))
     held = jnp.concatenate(parts, axis=0)
     return [held, swapped(held, "head", 1)], own
+
+
+def earlier_alike(devices):
+    blocks = devices.shape[-1]
+    same = devices[..., :, None] == devices[..., None, :]
+    before = np.tril(np.ones((blocks, blocks), bool), -1)
+    return jnp.sum(jnp.where(before, same, False).astype(jnp.int32), axis=-1)
+
+
+def split_kernel(room, index_ref, *refs):
+    count = 1 + index_ref.shape[0] // room
+    terms, outs = refs[:-count], refs[-count:]
+
+    def rows(where):
+        some = terms[0][where, :]
+        for term in terms[1:]:
+            some = some + term[where, :]
+        return some.astype(jnp.bfloat16)
+
+    outs[0][...] = rows(slice(None))
+    for r, out in enumerate(outs[1:]):
+        for c in range(room):
+            block = index_ref[r * room + c]
+            out[c * QB : (c + 1) * QB, :] = rows(pl.ds(pl.multiple_of(block * QB, QB), QB))
+
+
+def split(terms, index, room):
+    tokens, width = terms[0].shape
+    others = HOPS
+    vmem = pl.BlockSpec(memory_space=pltpu.VMEM)
+    return pl.pallas_call(
+        functools.partial(split_kernel, room),
+        out_shape=[jax.ShapeDtypeStruct((tokens, width), jnp.bfloat16)]
+        + [jax.ShapeDtypeStruct((room * QB, width), jnp.bfloat16)] * others,
+        in_specs=[pl.BlockSpec(memory_space=pltpu.SMEM)] + [vmem] * len(terms),
+        out_specs=[vmem] * (others + 1),
+        compiler_params=pltpu.CompilerParams(vmem_limit_bytes=16 * 2**20),
+    )(index, *terms)
+
+
+def exchanged(terms, destination, position, blocks):
+    group = HOPS + 1
+    room = blocks // 2
+    tokens = blocks * QB
+    place = position % group
+    slots = group * blocks
+    targets = lax.dynamic_slice_in_dim(destination, (position - place) * blocks, slots, 0)
+    order = place ^ np.arange(group, dtype=np.int32)
+    known = order[:, None] == np.arange(group, dtype=np.int32)[None, :]
+    slot = jnp.sum(
+        jnp.where(known[:, :, None], targets.reshape(1, group, blocks), 0), axis=1
+    )
+    device = slot // blocks % group
+    rank = earlier_alike(device)
+    places = np.arange(room, dtype=np.int32)
+    mine = (device[1:, None, :] == place) & (rank[1:, None, :] == places[None, :, None])
+    got = jnp.sum(jnp.where(mine, slot[1:, None, :] + 1, 0), axis=2) - 1
+    sent = (device[0][None, None, :] == order[1:, None, None]) & (
+        rank[0][None, None, :] == places[None, :, None]
+    )
+    numbers = np.arange(blocks, dtype=np.int32)
+    index = jnp.sum(jnp.where(sent, numbers[None, None, :], 0), axis=2).reshape(-1)
+    everywhere = (destination // blocks % group).reshape(-1, blocks)
+    few = jnp.max(earlier_alike(everywhere)) < room
+    tokens_here = position * tokens + jnp.arange(tokens, dtype=jnp.int32)
+
+    def placed(pieces, block_slots):
+        rows = (block_slots[:, None] * QB + np.arange(QB, dtype=np.int32)[None, :]).reshape(-1)
+        pick = (rows[:, None] == tokens_here[None, :]).astype(jnp.bfloat16)
+        return lax.dot_general(
+            jnp.concatenate(pieces, axis=0),
+            pick,
+            (((0,), (0,)), ((), ())),
+            preferred_element_type=jnp.float32,
+        ).astype(jnp.bfloat16)
+
+    def some(*terms):
+        own, *outgoing = split(terms, index, room)
+        pieces = [own] + [swapped(block, "ctx", r + 1) for r, block in enumerate(outgoing)]
+        return placed(pieces, jnp.concatenate([slot[0], got.reshape(-1)]))
+
+    def whole(*terms):
+        own = sum(terms[1:], terms[0]).astype(jnp.bfloat16)
+        pieces = [own] + [swapped(own, "ctx", r) for r in range(1, group)]
+        return placed(pieces, slot.reshape(-1))
+
+    return lax.cond(few, some, whole, *terms)
 
 
 def body(queries, kv_rows, doc_start, destination, out_weight):
@@ -394,30 +481,15 @@
     starts = lax.dynamic_slice_in_dim(doc_start, first, blocks, 0)
     own_rows = (first + jnp.arange(blocks, dtype=jnp.int32)) * QB
     inval = jnp.clip(starts - (own_rows - W1), 0, W1).astype(jnp.int32)
-    place = position % group
-    slots = group * blocks
-    targets = lax.dynamic_slice_in_dim(destination, first - place * blocks, slots, 0)
-    row = jnp.arange(group * tokens, dtype=jnp.int32)
-    source = (place ^ (row // tokens)) * blocks + row % tokens // QB
-    known = source[:, None] == jnp.arange(slots, dtype=jnp.int32)[None, :]
-    target = jnp.sum(jnp.where(known, targets[None, :], 0), axis=1) * QB + row % QB
-    pick = target[:, None] == (first * QB + jnp.arange(tokens, dtype=jnp.int32))[None, :]
-    pick = pick.astype(jnp.bfloat16)
     here = lax.axis_index("head").astype(jnp.int32)
     meta = jnp.concatenate([inval, here[None]])
     outputs = 2 if len(shards) == 2 else 1
     partials = attended_and_projected(own, shards, meta, out_weight, outputs)
     if outputs == 2:
-        summed = partials[1] + swapped(partials[0], "head", 1)
+        terms = [partials[1], swapped(partials[0], "head", 1)]
     else:
-        summed = lax.psum_scatter(partials[0], "head", scatter_dimension=1, tiled=True)
-    projected = summed.astype(jnp.bfloat16)
-    pieces = jnp.concatenate(
-        [projected] + [swapped(projected, "ctx", r) for r in range(1, group)], axis=0
-    )
-    return lax.dot_general(
-        pieces, pick, (((0,), (0,)), ((), ())), preferred_element_type=jnp.float32
-    ).astype(jnp.bfloat16)
+        terms = [lax.psum_scatter(partials[0], "head", scatter_dimension=1, tiled=True)]
+    return exchanged(terms, destination, position, blocks)
 
 
 def solution(mesh):

time: 186 us -> 182 us (0.978); the launches traced: 186 us -> 179 us
  waiting for transfers between devices: 14.8 us -> 7.48 us
  local copies, waits for them, and re-layouts: 6.42 us -> 3.33 us
  other arithmetic: 0.32 us -> 2.51 us
    ppermute x5, waiting for transfers between devices: 14.8 us -> 7.47 us  [swapped(): lax.ppermute(block, axis, [(i, i ^ bits) for i in range(lax.axis_size(axi...]
    unnamed x21 -> x15, local copies, waits for them, and re-layouts: 6.34 us -> 2.66 us
  transfers between devices with their start and end apart: 7 -> 7, of which waited for: 4 -> 4; matrix products, arithmetic and copies ran while one was open for 0% -> 1% of each run, Pallas kernels for 1% -> 1%
where the time goes in v4:
time: 182 us; the launch traced here: 179 us
  starting transfers between devices  123 us (68%)
  Pallas kernels  42.2 us (23%)
  waiting for transfers between devices  7.48 us (4%)
  local copies, waits for them, and re-layouts  3.33 us (2%)
  other arithmetic  2.51 us (1%)
    ppermute x5, starting transfers between devices, swapped(): lax.ppermute(block, axis, [(i, i ^ bits) for i in range(lax.axis_size(axi...  114 us
    pallas_call x1, Pallas kernels, attended_and_projected(): pl.pallas_call(functools.partial(attention_kernel, len(shards), outputs),...  39.9 us
    ppermute x2, starting transfers between devices, taken(): return lax.ppermute(kv_rows, ('ctx', 'head'), route)  8.4 us
    ppermute x5, waiting for transfers between devices, swapped(): lax.ppermute(block, axis, [(i, i ^ bits) for i in range(lax.axis_size(axi...  7.47 us
  transfers between devices with their start and end apart: 7, of which 4 were waited for; matrix products, arithmetic and copies ran while one was open for 1% of the time, Pallas kernels for 1%

profile of v4, /device:TPU:0, one launch (start us, length us, event | category | flops | bytes accessed | tf_op | source)
XLA Modules:
  0.0 179.4 jit_solution(13215525783183638550)
XLA Ops:
  0.0 5.0 %collective-permute-start.6 = (bf16[128,512]{1,0:T(8,128)(2,1)}, bf16[128,512]{1,0:T(8,128)(2,1)S(1)}, u32[]{:S(2)}, u32[]{:S(2)}) collective-permute-start(bf16[128,512]{1,0:T(8,128)(2,1)} %kv_ref.1), channel_id=1, source_target_pairs={{0,4},{2,6},{4,8},{1,9},{6,10},{3,11},{8,12},{5,13},{10,14},{7,15}... | collective-permute-start | bytes 393224 | tf_op jit(solution)/shard_map/ppermute | solution.py:379
  5.0 3.4 %collective-permute-start.7 = (bf16[128,512]{1,0:T(8,128)(2,1)}, bf16[128,512]{1,0:T(8,128)(2,1)S(1)}, u32[]{:S(2)}, u32[]{:S(2)}) collective-permute-start(bf16[128,512]{1,0:T(8,128)(2,1)} %kv_ref.1), channel_id=1, source_target_pairs={{0,2},{2,4},{4,6},{1,7},{6,8},{3,9},{8,10},{5,11},{10,12},{7,13},{... | collective-permute-start | bytes 393224 | tf_op jit(solution)/shard_map/ppermute | solution.py:379
  8.5 0.7 and_select_fusion.2
  9.2 1.0 copy-done
  10.2 0.9 copy-done.1
  11.1 1.0 shard_map.138
  12.3 0.1 convert_reduce_fusion
  12.5 0.4 collective-permute-start.8
  13.1 0.6 reduce_max.9
  14.5 39.9 %shard_map.139 = (f32[128,1024]{1,0:T(8,128)S(1)}, f32[128,1024]{1,0:T(8,128)}) custom-call(s32[5]{0:T(128)S(1)} %pad_add_fusion.meta_ref, f32[2048,128]{1,0:T(8,128)S(1)} %get-tuple-element.136.q3, bf16[128,128]{1,0:T(8,128)(2,1)S(1)} %get-tuple-element.137.k1o, bf16[1,144,128]{2,1,0:T(8,128)(2,1)S(1)} %get-tuple-element.138.v1o, ...), custom_call_target="tpu_custom_call" | custom-call | tf_op jit(solution)/shard_map/pallas_call | solution.py:333
  54.5 110.2 %collective-permute-start.9 = (f32[128,1024]{1,0:T(8,128)S(1)}, f32[128,1024]{1,0:T(8,128)S(1)}, u32[]{:S(2)}, u32[]{:S(2)}) collective-permute-start(f32[128,1024]{1,0:T(8,128)S(1)} %get-tuple-element.144), channel_id=1, source_target_pairs={{0,1},{1,0},{2,3},{3,2},{4,5},{5,4},{6,7},{7,6},{8,9},{9,8},{10,11... | collective-permute-start | bytes 1572872 | tf_op jit(solution)/shard_map/ppermute | solution.py:367
  164.8 1.4 collective-permute-done.9
  166.3 12.4 %conditional.2 = (bf16[1024,128]{1,0:T(8,128)(2,1)S(1)}) conditional(s32[]{:T(128)} %convert_element_type.20, (f32[128,1024]{1,0:T(8,128)}, f32[128,1024]{1,0:T(8,128)S(1)}, s32[4,4]{1,0:T(4,128)S(1)}, s32[1,32]{1,0:T(1,128)S(1)}, s32[128]{0:T(128)S(1)}) %tuple.25, (s32[4,4]{1,0:T(4,128)S(1)}, s32[4]{0:T(128)S(1)}, s32[4,4,4]{2,1,0:T(4,128)S(1)}, (), (), ...), branch_computations={%region_3.4_spmd, %region_4.8_spmd} | conditional | flops 138740240 | bytes 5776448
  166.3 0.1 reduce_sum.43
  166.6 0.2 fusion.23
  166.8 1.3 branch_1_fun.1
  168.2 2.1 %collective-permute-start.4 = (bf16[64,1024]{1,0:T(8,128)(2,1)S(1)}, bf16[64,1024]{1,0:T(8,128)(2,1)S(1)}, u32[]{:S(2)}, u32[]{:S(2)}) collective-permute-start(bf16[64,1024]{1,0:T(8,128)(2,1)S(1)} %get-tuple-element.110), channel_id=1, source_target_pairs={{0,4},{2,6},{4,0},{6,2},{8,12},{10,14},{12,8},{14,10},{16,20},{18,... | collective-permute-start | bytes 393224 | tf_op jit(solution)/shard_map/cond/branch_1_fun/ppermute | solution.py:367
  170.3 1.4 collective-permute-start.5
  171.7 0.1 fusion.24
  172.2 2.3 %collective-permute-done.3 = bf16[64,1024]{1,0:T(8,128)(2,1)S(1)} collective-permute-done((bf16[64,1024]{1,0:T(8,128)(2,1)S(1)}, bf16[64,1024]{1,0:T(8,128)(2,1)S(1)}, u32[]{:S(2)}, u32[]{:S(2)}) %collective-permute-start.3) | collective-permute-done | bytes 131104 | tf_op jit(solution)/shard_map/cond/branch_1_fun/ppermute | solution.py:367
  174.5 1.9 %collective-permute-done.4 = bf16[64,1024]{1,0:T(8,128)(2,1)S(1)} collective-permute-done((bf16[64,1024]{1,0:T(8,128)(2,1)S(1)}, bf16[64,1024]{1,0:T(8,128)(2,1)S(1)}, u32[]{:S(2)}, u32[]{:S(2)}) %collective-permute-start.4) | collective-permute-done | bytes 131104 | tf_op jit(solution)/shard_map/cond/branch_1_fun/ppermute | solution.py:367
  176.4 1.8 %collective-permute-done.5 = bf16[64,1024]{1,0:T(8,128)(2,1)S(1)} collective-permute-done((bf16[64,1024]{1,0:T(8,128)(2,1)S(1)}, bf16[64,1024]{1,0:T(8,128)(2,1)S(1)}, u32[]{:S(2)}, u32[]{:S(2)}) %collective-permute-start.5) | collective-permute-done | bytes 131104 | tf_op jit(solution)/shard_map/cond/branch_1_fun/ppermute | solution.py:367
  178.2 0.5 fusion.12
  178.7 0.7 copy-done.6
  (44 shorter events, 1.4 us)
Async XLA Ops:
  0.0 12.3 %copy-start.3 = (pred[4,4]{1,0:T(4,128)(4,1)S(1)}, pred[4,4]{1,0:T(4,128)(4,1)}, u32[]{:S(2)}) copy-start(pred[4,4]{1,0:T(4,128)(4,1)} %constant.103.clone) | copy-start | bytes 52
  0.0 12.4 %collective-permute-start.6 = (bf16[128,512]{1,0:T(8,128)(2,1)}, bf16[128,512]{1,0:T(8,128)(2,1)S(1)}, u32[]{:S(2)}, u32[]{:S(2)}) collective-permute-start(bf16[128,512]{1,0:T(8,128)(2,1)} %kv_ref.1), channel_id=1, source_target_pairs={{0,4},{2,6},{4,8},{1,9},{6,10},{3,11},{8,12},{5,13},{10,14},{7,15}... | collective-permute-start | bytes 393224 | tf_op jit(solution)/shard_map/ppermute | solution.py:379
  5.0 7.4 %collective-permute-start.7 = (bf16[128,512]{1,0:T(8,128)(2,1)}, bf16[128,512]{1,0:T(8,128)(2,1)S(1)}, u32[]{:S(2)}, u32[]{:S(2)}) collective-permute-start(bf16[128,512]{1,0:T(8,128)(2,1)} %kv_ref.1), channel_id=1, source_target_pairs={{0,2},{2,4},{4,6},{1,7},{6,8},{3,9},{8,10},{5,11},{10,12},{7,13},{... | collective-permute-start | bytes 393224 | tf_op jit(solution)/shard_map/ppermute | solution.py:379
  9.2 1.0 copy-start
  10.2 0.9 copy-start.1
  11.1 1.7 copy-start.4
  11.1 1.8 copy-start.5
  12.5 2.1 %collective-permute-start.8 = (bf16[256,512]{1,0:T(8,128)(2,1)S(1)}, bf16[256,512]{1,0:T(8,128)(2,1)S(1)}, u32[]{:S(2)}, u32[]{:S(2)}) collective-permute-start(bf16[256,512]{1,0:T(8,128)(2,1)S(1)} %constant_dynamic-update-slice_fusion.refs_0_), channel_id=1, source_target_pairs={{0,1},{1,0},{2,3},{3,2},{4,5},{5,4},{6,7},{7,6},{8,9},{9,8},{10,11... | collective-permute-start | bytes 786440 | tf_op jit(solution)/shard_map/ppermute | solution.py:367
  14.5 151.8 %copy-start.2 = (s32[1,32]{1,0:T(1,128)S(1)}, s32[1,32]{1,0:T(1,128)}, u32[]{:S(2)}) copy-start(s32[1,32]{1,0:T(1,128)} %constant.106.clone) | copy-start | bytes 388
  54.5 111.8 %collective-permute-start.9 = (f32[128,1024]{1,0:T(8,128)S(1)}, f32[128,1024]{1,0:T(8,128)S(1)}, u32[]{:S(2)}, u32[]{:S(2)}) collective-permute-start(f32[128,1024]{1,0:T(8,128)S(1)} %get-tuple-element.144), channel_id=1, source_target_pairs={{0,1},{1,0},{2,3},{3,2},{4,5},{5,4},{6,7},{7,6},{8,9},{9,8},{10,11... | collective-permute-start | bytes 1572872 | tf_op jit(solution)/shard_map/ppermute | solution.py:367
  168.1 6.4 %collective-permute-start.3 = (bf16[64,1024]{1,0:T(8,128)(2,1)S(1)}, bf16[64,1024]{1,0:T(8,128)(2,1)S(1)}, u32[]{:S(2)}, u32[]{:S(2)}) collective-permute-start(bf16[64,1024]{1,0:T(8,128)(2,1)S(1)} %get-tuple-element.109), channel_id=1, source_target_pairs={{0,2},{2,0},{4,6},{6,4},{8,10},{10,8},{12,14},{14,12},{16,18},{18,... | collective-permute-start | bytes 393224 | tf_op jit(solution)/shard_map/cond/branch_1_fun/ppermute | solution.py:367
  168.2 8.2 %collective-permute-start.4 = (bf16[64,1024]{1,0:T(8,128)(2,1)S(1)}, bf16[64,1024]{1,0:T(8,128)(2,1)S(1)}, u32[]{:S(2)}, u32[]{:S(2)}) collective-permute-start(bf16[64,1024]{1,0:T(8,128)(2,1)S(1)} %get-tuple-element.110), channel_id=1, source_target_pairs={{0,4},{2,6},{4,0},{6,2},{8,12},{10,14},{12,8},{14,10},{16,20},{18,... | collective-permute-start | bytes 393224 | tf_op jit(solution)/shard_map/cond/branch_1_fun/ppermute | solution.py:367
  170.3 7.9 %collective-permute-start.5 = (bf16[64,1024]{1,0:T(8,128)(2,1)S(1)}, bf16[64,1024]{1,0:T(8,128)(2,1)S(1)}, u32[]{:S(2)}, u32[]{:S(2)}) collective-permute-start(bf16[64,1024]{1,0:T(8,128)(2,1)S(1)} %get-tuple-element.111), channel_id=1, source_target_pairs={{0,6},{2,4},{4,2},{6,0},{8,14},{10,12},{12,10},{14,8},{16,22},{18,... | collective-permute-start | bytes 393224 | tf_op jit(solution)/shard_map/cond/branch_1_fun/ppermute | solution.py:367
  178.7 0.7 copy-start.6

commit v5 on v4

--- a/solution.py
+++ b/solution.py
@@ -17,6 +17,7 @@
 VR = DH + PACK
 SAMPLE = 32
 AHEAD = 3
+SPAN = 4
 LIMIT = 1e30
 LOG2E = 1.4426950408889634
 
@@ -68,6 +69,7 @@
     size = max(heads, PACK)
     pack = size // heads
     wide = min(2 * LANES, cols)
+    span = min(SPAN, QB // group)
     scale = LOG2E / np.sqrt(DH)
     f32, bf16 = jnp.float32, jnp.bfloat16
 
@@ -238,26 +240,28 @@
                 reset(b * QB, inv)
 
             def fast(s, _):
-                g = g0 + s
                 work = []
-                for u in range(group):
+                for u in range(span * group):
                     work += [(u, n) for n in range(0, cols, wide)]
-                source = {u: scores(g, u) for u in range(group)}
+                at = [divmod(u, group) for u in range(span * group)]
+                first = g0 + s * span
+                source = [scores(first + k, u) for k, u in at]
                 top = total = None
                 ahead = [next(source[u]) for u, n in work[:AHEAD]]
                 for i, (u, n) in enumerate(work):
                     if i + AHEAD < len(work):
                         ahead.append(next(source[work[i + AHEAD][0]]))
                     logits = ahead.pop(0)
+                    g, v = first + at[u][0], at[u][1]
                     if n == 0:
                         top = highest(logits[:SAMPLE]) * scale
                         total = None
-                    some = mix(g, u, n, logits, top)
+                    some = mix(g, v, n, logits, top)
                     total = some if total is None else total + some
                     if n + wide == cols:
-                        keep(g, u, total, top)
-                    if i == 0:
-                        finish(jnp.maximum(g - 1, 0))
+                        keep(g, v, total, top)
+                        if v == group // 2:
+                            finish(jnp.maximum(g - 1, 0))
                 return 0
 
             def slow(s, _):
@@ -274,7 +278,7 @@
 
             if exact:
                 return lax.fori_loop(0, QB, slow, 0)
-            return lax.fori_loop(0, QB // group, fast, 0)
+            return lax.fori_loop(0, QB // group // span, fast, 0)
 
         lax.fori_loop(0, tokens // QB, block, 0)
         if exact:
@@ -374,7 +378,7 @@
     def taken(distances):
         devices = range(lax.axis_size("ctx"))
         route = [
-            ((i - d) * 2 + h, i * 2 + h) for i in devices for h, d in enumerate(distances) if i >= d
+            ((i - d) % len(devices) * 2 + h, i * 2 + h) for i in devices for h, d in enumerate(distances)
         ]
         return lax.ppermute(kv_rows, ("ctx", "head"), route)
 

time: 182 us -> 174 us (0.956); the launches traced: 179 us -> 175 us
  Pallas kernels: 42.2 us -> 38.2 us
  starting transfers between devices: 123 us -> 119 us
  waiting for transfers between devices: 7.48 us -> 11.1 us
    ppermute x2, waiting for transfers between devices: 0.01 us -> 5.02 us  [taken(): return lax.ppermute(kv_rows, ('ctx', 'head'), route)]
    pallas_call x1, Pallas kernels: 39.9 us -> 35.9 us  [attended_and_projected(): pl.pallas_call(functools.partial(attention_kernel, len(shards), outputs),...]
    ppermute x2, starting transfers between devices: 8.4 us -> 4.46 us  [taken(): return lax.ppermute(kv_rows, ('ctx', 'head'), route)]
  transfers between devices with their start and end apart: 7 -> 7, of which waited for: 4 -> 5; matrix products, arithmetic and copies ran while one was open for 1% -> 2% of each run, Pallas kernels for 1% -> 1%
where the time goes in v5:
time: 174 us; the launch traced here: 175 us
  starting transfers between devices  119 us (68%)
  Pallas kernels  38.2 us (22%)
  waiting for transfers between devices  11.1 us (6%)
  local copies, waits for them, and re-layouts  3.32 us (2%)
  other arithmetic  2.52 us (1%)
    ppermute x5, starting transfers between devices, swapped(): lax.ppermute(block, axis, [(i, i ^ bits) for i in range(lax.axis_size(axi...  114 us
    pallas_call x1, Pallas kernels, attended_and_projected(): pl.pallas_call(functools.partial(attention_kernel, len(shards), outputs),...  35.9 us
    ppermute x5, waiting for transfers between devices, swapped(): lax.ppermute(block, axis, [(i, i ^ bits) for i in range(lax.axis_size(axi...  6.1 us
    ppermute x2, waiting for transfers between devices, taken(): return lax.ppermute(kv_rows, ('ctx', 'head'), route)  5.02 us
    ppermute x2, starting transfers between devices, taken(): return lax.ppermute(kv_rows, ('ctx', 'head'), route)  4.46 us
  transfers between devices with their start and end apart: 7, of which 5 were waited for; matrix products, arithmetic and copies ran while one was open for 2% of the time, Pallas kernels for 1%

profile of v5, /device:TPU:0, one launch (start us, length us, event | category | flops | bytes accessed | tf_op | source)
XLA Modules:
  0.0 175.0 jit_solution(8657772536105143726)
XLA Ops:
  0.0 3.0 %collective-permute-start.6 = (bf16[128,512]{1,0:T(8,128)(2,1)}, bf16[128,512]{1,0:T(8,128)(2,1)S(1)}, u32[]{:S(2)}, u32[]{:S(2)}) collective-permute-start(bf16[128,512]{1,0:T(8,128)(2,1)} %kv_ref.1), channel_id=1, source_target_pairs={{28,0},{25,1},{30,2},{27,3},{0,4},{29,5},{2,6},{31,7},{4,8},{1,9},... | collective-permute-start | bytes 393224 | tf_op jit(solution)/shard_map/ppermute | solution.py:383
  3.0 1.5 collective-permute-start.7
  4.5 0.7 and_select_fusion.2
  5.2 1.0 copy-done
  6.3 0.9 copy-done.1
  7.2 1.0 shard_map.138
  8.3 0.1 convert_reduce_fusion
  8.4 1.9 %collective-permute-done.6 = bf16[128,512]{1,0:T(8,128)(2,1)S(1)} collective-permute-done((bf16[128,512]{1,0:T(8,128)(2,1)}, bf16[128,512]{1,0:T(8,128)(2,1)S(1)}, u32[]{:S(2)}, u32[]{:S(2)}) %collective-permute-start.6) | collective-permute-done | bytes 131104 | tf_op jit(solution)/shard_map/ppermute | solution.py:383
  10.4 3.1 %collective-permute-done.7 = bf16[128,512]{1,0:T(8,128)(2,1)S(1)} collective-permute-done((bf16[128,512]{1,0:T(8,128)(2,1)}, bf16[128,512]{1,0:T(8,128)(2,1)S(1)}, u32[]{:S(2)}, u32[]{:S(2)}) %collective-permute-start.7) | collective-permute-done | bytes 131104 | tf_op jit(solution)/shard_map/ppermute | solution.py:383
  13.8 0.6 reduce_max.9
  15.2 0.1 select_reduce_fusion
  15.3 35.9 %shard_map.139 = (f32[128,1024]{1,0:T(8,128)S(1)}, f32[128,1024]{1,0:T(8,128)}) custom-call(s32[5]{0:T(128)S(1)} %pad_add_fusion.meta_ref, f32[2048,128]{1,0:T(8,128)S(1)} %get-tuple-element.136.q3, bf16[128,128]{1,0:T(8,128)(2,1)S(1)} %get-tuple-element.137.k1o, bf16[1,144,128]{2,1,0:T(8,128)(2,1)S(1)} %get-tuple-element.138.v1o, ...), custom_call_target="tpu_custom_call" | custom-call | tf_op jit(solution)/shard_map/pallas_call | solution.py:337
  51.2 110.5 %collective-permute-start.9 = (f32[128,1024]{1,0:T(8,128)S(1)}, f32[128,1024]{1,0:T(8,128)S(1)}, u32[]{:S(2)}, u32[]{:S(2)}) collective-permute-start(f32[128,1024]{1,0:T(8,128)S(1)} %get-tuple-element.144), channel_id=1, source_target_pairs={{0,1},{1,0},{2,3},{3,2},{4,5},{5,4},{6,7},{7,6},{8,9},{9,8},{10,11... | collective-permute-start | bytes 1572872 | tf_op jit(solution)/shard_map/ppermute | solution.py:371
  161.8 1.4 collective-permute-done.9
  163.3 11.1 %conditional.2 = (bf16[1024,128]{1,0:T(8,128)(2,1)S(1)}) conditional(s32[]{:T(128)} %convert_element_type.20, (f32[128,1024]{1,0:T(8,128)}, f32[128,1024]{1,0:T(8,128)S(1)}, s32[4,4]{1,0:T(4,128)S(1)}, s32[1,32]{1,0:T(1,128)S(1)}, s32[128]{0:T(128)S(1)}) %tuple.25, (s32[4,4]{1,0:T(4,128)S(1)}, s32[4]{0:T(128)S(1)}, s32[4,4,4]{2,1,0:T(4,128)S(1)}, (), (), ...), branch_computations={%region_3.4_spmd, %region_4.8_spmd} | conditional | flops 138740240 | bytes 5776448
  163.3 0.1 reduce_sum.43
  163.6 0.2 fusion.23
  163.8 1.3 branch_1_fun.1
  165.3 3.4 %collective-permute-start.5 = (bf16[64,1024]{1,0:T(8,128)(2,1)S(1)}, bf16[64,1024]{1,0:T(8,128)(2,1)S(1)}, u32[]{:S(2)}, u32[]{:S(2)}) collective-permute-start(bf16[64,1024]{1,0:T(8,128)(2,1)S(1)} %get-tuple-element.111), channel_id=1, source_target_pairs={{0,6},{2,4},{4,2},{6,0},{8,14},{10,12},{12,10},{14,8},{16,22},{18,... | collective-permute-start | bytes 393224 | tf_op jit(solution)/shard_map/cond/branch_1_fun/ppermute | solution.py:371
  168.7 0.1 fusion.24
  169.2 2.3 %collective-permute-done.3 = bf16[64,1024]{1,0:T(8,128)(2,1)S(1)} collective-permute-done((bf16[64,1024]{1,0:T(8,128)(2,1)S(1)}, bf16[64,1024]{1,0:T(8,128)(2,1)S(1)}, u32[]{:S(2)}, u32[]{:S(2)}) %collective-permute-start.3) | collective-permute-done | bytes 131104 | tf_op jit(solution)/shard_map/cond/branch_1_fun/ppermute | solution.py:371
  171.5 2.3 %collective-permute-done.4 = bf16[64,1024]{1,0:T(8,128)(2,1)S(1)} collective-permute-done((bf16[64,1024]{1,0:T(8,128)(2,1)S(1)}, bf16[64,1024]{1,0:T(8,128)(2,1)S(1)}, u32[]{:S(2)}, u32[]{:S(2)}) %collective-permute-start.4) | collective-permute-done | bytes 131104 | tf_op jit(solution)/shard_map/cond/branch_1_fun/ppermute | solution.py:371
  173.8 0.5 fusion.12
  174.3 0.7 copy-done.6
  (44 shorter events, 1.5 us)
Async XLA Ops:
  0.0 8.3 %copy-start.3 = (pred[4,4]{1,0:T(4,128)(4,1)S(1)}, pred[4,4]{1,0:T(4,128)(4,1)}, u32[]{:S(2)}) copy-start(pred[4,4]{1,0:T(4,128)(4,1)} %constant.103.clone) | copy-start | bytes 52
  0.0 10.4 %collective-permute-start.6 = (bf16[128,512]{1,0:T(8,128)(2,1)}, bf16[128,512]{1,0:T(8,128)(2,1)S(1)}, u32[]{:S(2)}, u32[]{:S(2)}) collective-permute-start(bf16[128,512]{1,0:T(8,128)(2,1)} %kv_ref.1), channel_id=1, source_target_pairs={{28,0},{25,1},{30,2},{27,3},{0,4},{29,5},{2,6},{31,7},{4,8},{1,9},... | collective-permute-start | bytes 393224 | tf_op jit(solution)/shard_map/ppermute | solution.py:383
  3.0 10.5 %collective-permute-start.7 = (bf16[128,512]{1,0:T(8,128)(2,1)}, bf16[128,512]{1,0:T(8,128)(2,1)S(1)}, u32[]{:S(2)}, u32[]{:S(2)}) collective-permute-start(bf16[128,512]{1,0:T(8,128)(2,1)} %kv_ref.1), channel_id=1, source_target_pairs={{30,0},{27,1},{0,2},{29,3},{2,4},{31,5},{4,6},{1,7},{6,8},{3,9},{8... | collective-permute-start | bytes 393224 | tf_op jit(solution)/shard_map/ppermute | solution.py:383
  5.2 1.0 copy-start
  6.3 0.9 copy-start.1
  7.2 6.4 %copy-start.4 = (s32[64]{0:T(128)S(1)}, s32[64]{0:T(128)}, u32[]{:S(2)}) copy-start(s32[64]{0:T(128)} %param.18) | copy-start | bytes 772
  7.2 6.5 %copy-start.5 = (s32[64]{0:T(128)S(1)}, s32[64]{0:T(128)}, u32[]{:S(2)}) copy-start(s32[64]{0:T(128)} %param.19) | copy-start | bytes 772
  13.5 1.8 %collective-permute-start.8 = (bf16[256,512]{1,0:T(8,128)(2,1)S(1)}, bf16[256,512]{1,0:T(8,128)(2,1)S(1)}, u32[]{:S(2)}, u32[]{:S(2)}) collective-permute-start(bf16[256,512]{1,0:T(8,128)(2,1)S(1)} %constant_dynamic-update-slice_fusion.refs_0_), channel_id=1, source_target_pairs={{0,1},{1,0},{2,3},{3,2},{4,5},{5,4},{6,7},{7,6},{8,9},{9,8},{10,11... | collective-permute-start | bytes 786440 | tf_op jit(solution)/shard_map/ppermute | solution.py:371
  15.3 148.0 %copy-start.2 = (s32[1,32]{1,0:T(1,128)S(1)}, s32[1,32]{1,0:T(1,128)}, u32[]{:S(2)}) copy-start(s32[1,32]{1,0:T(1,128)} %constant.106.clone) | copy-start | bytes 388
  51.2 112.0 %collective-permute-start.9 = (f32[128,1024]{1,0:T(8,128)S(1)}, f32[128,1024]{1,0:T(8,128)S(1)}, u32[]{:S(2)}, u32[]{:S(2)}) collective-permute-start(f32[128,1024]{1,0:T(8,128)S(1)} %get-tuple-element.144), channel_id=1, source_target_pairs={{0,1},{1,0},{2,3},{3,2},{4,5},{5,4},{6,7},{7,6},{8,9},{9,8},{10,11... | collective-permute-start | bytes 1572872 | tf_op jit(solution)/shard_map/ppermute | solution.py:371
  165.1 6.4 %collective-permute-start.3 = (bf16[64,1024]{1,0:T(8,128)(2,1)S(1)}, bf16[64,1024]{1,0:T(8,128)(2,1)S(1)}, u32[]{:S(2)}, u32[]{:S(2)}) collective-permute-start(bf16[64,1024]{1,0:T(8,128)(2,1)S(1)} %get-tuple-element.109), channel_id=1, source_target_pairs={{0,2},{2,0},{4,6},{6,4},{8,10},{10,8},{12,14},{14,12},{16,18},{18,... | collective-permute-start | bytes 393224 | tf_op jit(solution)/shard_map/cond/branch_1_fun/ppermute | solution.py:371
  165.2 8.7 %collective-permute-start.4 = (bf16[64,1024]{1,0:T(8,128)(2,1)S(1)}, bf16[64,1024]{1,0:T(8,128)(2,1)S(1)}, u32[]{:S(2)}, u32[]{:S(2)}) collective-permute-start(bf16[64,1024]{1,0:T(8,128)(2,1)S(1)} %get-tuple-element.110), channel_id=1, source_target_pairs={{0,4},{2,6},{4,0},{6,2},{8,12},{10,14},{12,8},{14,10},{16,20},{18,... | collective-permute-start | bytes 393224 | tf_op jit(solution)/shard_map/cond/branch_1_fun/ppermute | solution.py:371
  165.3 8.6 %collective-permute-start.5 = (bf16[64,1024]{1,0:T(8,128)(2,1)S(1)}, bf16[64,1024]{1,0:T(8,128)(2,1)S(1)}, u32[]{:S(2)}, u32[]{:S(2)}) collective-permute-start(bf16[64,1024]{1,0:T(8,128)(2,1)S(1)} %get-tuple-element.111), channel_id=1, source_target_pairs={{0,6},{2,4},{4,2},{6,0},{8,14},{10,12},{12,10},{14,8},{16,22},{18,... | collective-permute-start | bytes 393224 | tf_op jit(solution)/shard_map/cond/branch_1_fun/ppermute | solution.py:371
  174.3 0.7 copy-start.6

commit v6 on v3

--- a/solution.py
+++ b/solution.py
@@ -17,6 +17,7 @@
 VR = DH + PACK
 SAMPLE = 32
 AHEAD = 3
+SPAN = 4
 LIMIT = 1e30
 LOG2E = 1.4426950408889634
 
@@ -68,6 +69,7 @@
     size = max(heads, PACK)
     pack = size // heads
     wide = min(2 * LANES, cols)
+    span = min(SPAN, QB // group)
     scale = LOG2E / np.sqrt(DH)
     f32, bf16 = jnp.float32, jnp.bfloat16
 
@@ -224,7 +226,8 @@
             ]
             shift *= 2
         value = sums[0][:DH] * (1.0 / sums[0][DH : DH + 1])
-        rows[pl.ds(pl.multiple_of(g * LANES, LANES), LANES), :] = value.T
+        spot = (meta_ref[blocks + 1 + g * group // QB] * QB + g * group % QB) * heads
+        rows[pl.ds(pl.multiple_of(spot, LANES), LANES), :] = value.T
 
     def run(exact):
         prepare()
@@ -238,26 +241,28 @@
                 reset(b * QB, inv)
 
             def fast(s, _):
-                g = g0 + s
                 work = []
-                for u in range(group):
+                for u in range(span * group):
                     work += [(u, n) for n in range(0, cols, wide)]
-                source = {u: scores(g, u) for u in range(group)}
+                at = [divmod(u, group) for u in range(span * group)]
+                first = g0 + s * span
+                source = [scores(first + k, u) for k, u in at]
                 top = total = None
                 ahead = [next(source[u]) for u, n in work[:AHEAD]]
                 for i, (u, n) in enumerate(work):
                     if i + AHEAD < len(work):
                         ahead.append(next(source[work[i + AHEAD][0]]))
                     logits = ahead.pop(0)
+                    g, v = first + at[u][0], at[u][1]
                     if n == 0:
                         top = highest(logits[:SAMPLE]) * scale
                         total = None
-                    some = mix(g, u, n, logits, top)
+                    some = mix(g, v, n, logits, top)
                     total = some if total is None else total + some
                     if n + wide == cols:
-                        keep(g, u, total, top)
-                    if i == 0:
-                        finish(jnp.maximum(g - 1, 0))
+                        keep(g, v, total, top)
+                        if v == group // 2:
+                            finish(jnp.maximum(g - 1, 0))
                 return 0
 
             def slow(s, _):
@@ -274,7 +279,7 @@
 
             if exact:
                 return lax.fori_loop(0, QB, slow, 0)
-            return lax.fori_loop(0, QB // group, fast, 0)
+            return lax.fori_loop(0, QB // group // span, fast, 0)
 
         lax.fori_loop(0, tokens // QB, block, 0)
         if exact:
@@ -297,7 +302,8 @@
         begin = 0 if outputs == 1 else jnp.where(here == k, width, 0)
         for n in range(0, width, step):
             some = wbuf[:, pl.ds(pl.multiple_of(begin + n, step), step)]
-            out_ref[:, n : n + step] = jnp.dot(attended, some, preferred_element_type=f32)
+            some = jnp.dot(attended, some, preferred_element_type=f32)
+            out_ref[:, n : n + step] = some.astype(out_ref.dtype)
 
 
 VMEM = pl.BlockSpec(memory_space=pltpu.VMEM)
@@ -332,7 +338,10 @@
     f32, bf16 = jnp.float32, jnp.bfloat16
     return pl.pallas_call(
         functools.partial(attention_kernel, len(shards), outputs),
-        out_shape=[jax.ShapeDtypeStruct((tokens, weight.shape[1] // outputs), f32)] * outputs,
+        out_shape=[
+            jax.ShapeDtypeStruct((tokens, weight.shape[1] // outputs), kind)
+            for kind in (bf16, f32)[2 - outputs :]
+        ],
         in_specs=[pl.BlockSpec(memory_space=pltpu.SMEM)] + [VMEM] * 5 + [HBM] + [VMEM] * len(shards),
         out_specs=[VMEM] * outputs,
         scratch_shapes=[
@@ -352,7 +361,7 @@
             pltpu.VMEM((8, LANES), f32),
             pltpu.VMEM((tokens * heads, DH), f32),
         ],
-        compiler_params=pltpu.CompilerParams(vmem_limit_bytes=46 * 2**20),
+        compiler_params=pltpu.CompilerParams(vmem_limit_bytes=43 * 2**20),
     )(meta, *own, weight, *shards)
 
 HOPS = 3
@@ -374,13 +383,93 @@
     def taken(distances):
         devices = range(lax.axis_size("ctx"))
         route = [
-            ((i - d) * 2 + h, i * 2 + h) for i in devices for h, d in enumerate(distances) if i >= d
+            ((i - d) % len(devices) * 2 + h, i * 2 + h) for i in devices for h, d in enumerate(distances)
         ]
         return lax.ppermute(kv_rows, ("ctx", "head"), route)
 
     parts, own = lax.optimization_barrier(([taken((2, 4)), taken((1, 3))], own))
     held = jnp.concatenate(parts, axis=0)
     return [held, swapped(held, "head", 1)], own
+
+
+def sorted_places(keys):
+    blocks = keys.shape[-1]
+    before = np.tril(np.ones((blocks, blocks), bool), -1)
+    mine, other = keys[..., :, None], keys[..., None, :]
+    return jnp.sum(((other < mine) | ((other == mine) & before)).astype(jnp.int32), axis=-1)
+
+
+class Exchange:
+    def __init__(self, destination, position, blocks):
+        group = HOPS + 1
+        self.blocks, self.room = blocks, blocks // 2
+        self.position = position
+        place = position % group
+        near = lax.dynamic_slice_in_dim(destination, (position - place) * blocks, group * blocks, 0)
+        order = place ^ np.arange(group, dtype=np.int32)
+        known = order[:, None] == np.arange(group, dtype=np.int32)[None, :]
+        slot = jnp.sum(jnp.where(known[:, :, None], near.reshape(1, group, blocks), 0), axis=1)
+        distance = (slot // blocks % group) ^ order[:, None]
+        places = sorted_places(distance)
+        self.places = places[0]
+        numbers = np.arange(blocks, dtype=np.int32)
+        here = places[:, None, :] == numbers[None, :, None]
+        slots = jnp.sum(jnp.where(here, slot[:, None, :], 0), axis=2)
+
+        def starts(distances, limits):
+            nearer = jnp.sum((distances < limits[:, None]).astype(jnp.int32), axis=1)
+            return jnp.minimum(nearer, blocks - self.room)
+
+        swaps = np.arange(1, group, dtype=np.int32)
+        start = starts(distance[:1], swaps)
+        first = starts(distance[1:], swaps)[:, None, None]
+        window = first + np.arange(self.room, dtype=np.int32)[None, :, None] == numbers[None, None, :]
+        got = jnp.sum(jnp.where(window, slots[1:, None, :], 0), axis=2)
+        to = (destination // blocks % group).reshape(-1, blocks)
+        counts = jnp.sum((to[:, :, None] == to[:, None, :]).astype(jnp.int32), axis=2)
+        few = jnp.max(counts) <= self.room
+
+        def rows(slots):
+            return (slots[:, None] * QB + np.arange(QB, dtype=np.int32)[None, :]).reshape(-1)
+
+        self.plan = (
+            [start[r] for r in range(HOPS)],
+            rows(jnp.concatenate([slots[0], got.reshape(-1)])),
+            rows(slots.reshape(-1)),
+            few,
+        )
+
+    def placed(self, pieces, rows):
+        tokens = self.blocks * QB
+        stored = self.position * tokens + jnp.arange(tokens, dtype=jnp.int32)
+        pick = (rows[:, None] == stored[None, :]).astype(jnp.bfloat16)
+        return lax.dot_general(
+            jnp.concatenate(pieces, axis=0),
+            pick,
+            (((0,), (0,)), ((), ())),
+            preferred_element_type=jnp.float32,
+        ).astype(jnp.bfloat16)
+
+    def __call__(self, terms, plan):
+        start, some_rows, whole_rows, few = plan
+
+        def added(terms):
+            return sum((term.astype(jnp.float32) for term in terms[1:]), terms[0]).astype(jnp.bfloat16)
+
+        def some(*terms):
+            own = added(terms)
+            pieces = [own]
+            for r in range(HOPS):
+                rows = lax.dynamic_slice_in_dim(own, start[r] * QB, self.room * QB, 0)
+                pieces.append(swapped(rows, "ctx", r + 1))
+            return self.placed(pieces, some_rows)
+
+        def whole(*terms):
+            own = added(terms)
+            pieces = [own] + [swapped(own, "ctx", r) for r in range(1, HOPS + 1)]
+            return self.placed(pieces, whole_rows)
+
+        return lax.cond(few, some, whole, *terms)
 
 
 def body(queries, kv_rows, doc_start, destination, out_weight):
@@ -394,30 +483,17 @@
     starts = lax.dynamic_slice_in_dim(doc_start, first, blocks, 0)
     own_rows = (first + jnp.arange(blocks, dtype=jnp.int32)) * QB
     inval = jnp.clip(starts - (own_rows - W1), 0, W1).astype(jnp.int32)
-    place = position % group
-    slots = group * blocks
-    targets = lax.dynamic_slice_in_dim(destination, first - place * blocks, slots, 0)
-    row = jnp.arange(group * tokens, dtype=jnp.int32)
-    source = (place ^ (row // tokens)) * blocks + row % tokens // QB
-    known = source[:, None] == jnp.arange(slots, dtype=jnp.int32)[None, :]
-    target = jnp.sum(jnp.where(known, targets[None, :], 0), axis=1) * QB + row % QB
-    pick = target[:, None] == (first * QB + jnp.arange(tokens, dtype=jnp.int32))[None, :]
-    pick = pick.astype(jnp.bfloat16)
     here = lax.axis_index("head").astype(jnp.int32)
-    meta = jnp.concatenate([inval, here[None]])
+    exchange = Exchange(destination, position, blocks)
+    meta = jnp.concatenate([inval, here[None], exchange.places])
     outputs = 2 if len(shards) == 2 else 1
     partials = attended_and_projected(own, shards, meta, out_weight, outputs)
+    partials, plan = lax.optimization_barrier((partials, exchange.plan))
     if outputs == 2:
-        summed = partials[1] + swapped(partials[0], "head", 1)
+        terms = [partials[1], swapped(partials[0], "head", 1)]
     else:
-        summed = lax.psum_scatter(partials[0], "head", scatter_dimension=1, tiled=True)
-    projected = summed.astype(jnp.bfloat16)
-    pieces = jnp.concatenate(
-        [projected] + [swapped(projected, "ctx", r) for r in range(1, group)], axis=0
-    )
-    return lax.dot_general(
-        pieces, pick, (((0,), (0,)), ((), ())), preferred_element_type=jnp.float32
-    ).astype(jnp.bfloat16)
+        terms = [lax.psum_scatter(partials[0], "head", scatter_dimension=1, tiled=True)]
+    return exchange(terms, plan)
 
 
 def solution(mesh):

time: 186 us -> 178 us (0.957)
  waiting for transfers between devices: 14.8 us -> 9.09 us
  other arithmetic: 0.32 us -> 5.24 us
  starting transfers between devices: 123 us -> 119 us
  Pallas kernels: 40.8 us -> 37 us
    ppermute x5, waiting for transfers between devices: 14.8 us -> 7.64 us  [swapped(): lax.ppermute(block, axis, [(i, i ^ bits) for i in range(lax.axis_size(axi...]
    ppermute x2, starting transfers between devices: 8.27 us -> 4.46 us  [taken(): return lax.ppermute(kv_rows, ('ctx', 'head'), route)]
    pallas_call x1, Pallas kernels: 39.8 us -> 36 us  [attended_and_projected(): pl.pallas_call(functools.partial(attention_kernel, len(shards), outputs),...]
    unnamed x21 -> x9, local copies, waits for them, and re-layouts: 6.34 us -> 2.67 us
    reduce_sum x1 -> x6, other arithmetic: 0.09 us -> 2.22 us  [the longest x1 0.87 us: sorted_places(): jnp.sum(((other < mine) | (other == mine) & before).astype(jnp.int32), ax...]
  transfers between devices with their start and end apart: 7 -> 7, of which waited for: 4 -> 5; matrix products, arithmetic and copies ran while one was open for 0% -> 3% of each run, Pallas kernels for 1% -> 1%
where the time goes in v6:
time: 178 us
  starting transfers between devices  119 us (67%)
  Pallas kernels  37 us (21%)
  waiting for transfers between devices  9.09 us (5%)
  other arithmetic  5.24 us (3%)
  local copies, waits for them, and re-layouts  4.69 us (3%)
  loops' own time  1.85 us (1%)
    ppermute x5, starting transfers between devices, swapped(): lax.ppermute(block, axis, [(i, i ^ bits) for i in range(lax.axis_size(axi...  114 us
    pallas_call x1, Pallas kernels, attended_and_projected(): pl.pallas_call(functools.partial(attention_kernel, len(shards), outputs),...  36 us
    ppermute x5, waiting for transfers between devices, swapped(): lax.ppermute(block, axis, [(i, i ^ bits) for i in range(lax.axis_size(axi...  7.64 us
    ppermute x2, starting transfers between devices, taken(): return lax.ppermute(kv_rows, ('ctx', 'head'), route)  4.46 us
  transfers between devices with their start and end apart: 7, of which 5 were waited for; matrix products, arithmetic and copies ran while one was open for 3% of the time, Pallas kernels for 1%

profile of v6, /device:TPU:0, one launch (start us, length us, event | category | flops | bytes accessed | tf_op | source)
XLA Modules:
  0.0 177.7 jit_solution(16624466011931288917)
XLA Ops:
  0.0 3.0 %collective-permute-start.6 = (bf16[128,512]{1,0:T(8,128)(2,1)}, bf16[128,512]{1,0:T(8,128)(2,1)S(1)}, u32[]{:S(2)}, u32[]{:S(2)}) collective-permute-start(bf16[128,512]{1,0:T(8,128)(2,1)} %kv_ref.1), channel_id=1, source_target_pairs={{28,0},{25,1},{30,2},{27,3},{0,4},{29,5},{2,6},{31,7},{4,8},{1,9},... | collective-permute-start | bytes 393224 | tf_op jit(solution)/shard_map/ppermute | solution.py:388
  3.0 1.5 collective-permute-start.7
  4.5 0.7 and_select_fusion
  5.1 0.7 dynamic_slice.16
  6.2 0.9 convert_reduce_fusion.1
  7.3 0.9 convert_reduce_fusion.2
  8.8 1.1 copy-done
  9.9 0.9 copy-done.1
  10.8 1.0 shard_map.145
  12.0 1.4 collective-permute-done.7
  13.8 0.6 reduce_max.9
  15.2 0.7 fusion.30
  15.8 36.0 %shard_map.146 = (bf16[128,1024]{1,0:T(8,128)(2,1)}, f32[128,1024]{1,0:T(8,128)}) custom-call(s32[9]{0:T(128)S(1)} %pad_add_fusion.meta_ref, f32[2048,128]{1,0:T(8,128)S(1)} %get-tuple-element.70.q3, bf16[128,128]{1,0:T(8,128)(2,1)S(1)} %get-tuple-element.71.k1o, bf16[1,144,128]{2,1,0:T(8,128)(2,1)S(1)} %get-tuple-element.72.v1o, ...), custom_call_target="tpu_custom_call" | custom-call | tf_op jit(solution)/shard_map/pallas_call | solution.py:339
  51.9 110.5 %collective-permute-start.9 = (bf16[128,1024]{1,0:T(8,128)(2,1)}, bf16[128,1024]{1,0:T(8,128)(2,1)S(1)}, u32[]{:S(2)}, u32[]{:S(2)}) collective-permute-start(bf16[128,1024]{1,0:T(8,128)(2,1)} %get-tuple-element.80), channel_id=1, source_target_pairs={{0,1},{1,0},{2,3},{3,2},{4,5},{5,4},{6,7},{7,6},{8,9},{9,8},{10,11... | collective-permute-start | bytes 786440 | tf_op jit(solution)/shard_map/ppermute | solution.py:376
  162.4 1.4 collective-permute-done.9
  163.7 13.3 %conditional.2 = (bf16[1024,128]{1,0:T(8,128)(2,1)S(1)}) conditional(s32[]{:T(128)} %convert_element_type.38, (bf16[128,1024]{1,0:T(8,128)(2,1)S(1)}, f32[128,1024]{1,0:T(8,128)}, s32[512]{0:T(512)S(1)}, s32[]{:T(128)}) %tuple.18, (bf16[128,1024]{1,0:T(8,128)(2,1)S(1)}, f32[128,1024]{1,0:T(8,128)}, s32[]{:T(128)}, s32[]{:T(128)}, s32[]{:T(128)}, ...), branch_computations={%region_8.9_spmd, %region_9.10_spmd} | conditional | flops 138870912 | bytes 5508240
  165.5 1.1 add_convert_fusion.1
  166.8 0.9 collective-permute-start.5
  167.7 2.6 %collective-permute-start.4 = (bf16[64,1024]{1,0:T(8,128)(2,1)S(1)}, bf16[64,1024]{1,0:T(8,128)(2,1)S(1)}, u32[]{:S(2)}, u32[]{:S(2)}) collective-permute-start(bf16[64,1024]{1,0:T(8,128)(2,1)S(1)} %get-tuple-element.91), channel_id=1, source_target_pairs={{0,4},{2,6},{4,0},{6,2},{8,12},{10,14},{12,8},{14,10},{16,20},{18,... | collective-permute-start | bytes 393224 | tf_op jit(solution)/shard_map/cond/branch_1_fun/ppermute | solution.py:376
  170.3 2.8 %collective-permute-done.3 = bf16[64,1024]{1,0:T(8,128)(2,1)S(1)} collective-permute-done((bf16[64,1024]{1,0:T(8,128)(2,1)S(1)}, bf16[64,1024]{1,0:T(8,128)(2,1)S(1)}, u32[]{:S(2)}, u32[]{:S(2)}) %collective-permute-start.3) | collective-permute-done | bytes 131104 | tf_op jit(solution)/shard_map/cond/branch_1_fun/ppermute | solution.py:376
  173.1 1.3 collective-permute-done.5
  174.3 2.2 %collective-permute-done.4 = bf16[64,1024]{1,0:T(8,128)(2,1)S(1)} collective-permute-done((bf16[64,1024]{1,0:T(8,128)(2,1)S(1)}, bf16[64,1024]{1,0:T(8,128)(2,1)S(1)}, u32[]{:S(2)}, u32[]{:S(2)}) %collective-permute-start.4) | collective-permute-done | bytes 131104 | tf_op jit(solution)/shard_map/cond/branch_1_fun/ppermute | solution.py:376
  176.5 0.5 fusion.12
  177.0 0.7 copy-done.3
  (39 shorter events, 1.9 us)
Async XLA Ops:
  0.0 12.0 %collective-permute-start.6 = (bf16[128,512]{1,0:T(8,128)(2,1)}, bf16[128,512]{1,0:T(8,128)(2,1)S(1)}, u32[]{:S(2)}, u32[]{:S(2)}) collective-permute-start(bf16[128,512]{1,0:T(8,128)(2,1)} %kv_ref.1), channel_id=1, source_target_pairs={{28,0},{25,1},{30,2},{27,3},{0,4},{29,5},{2,6},{31,7},{4,8},{1,9},... | collective-permute-start | bytes 393224 | tf_op jit(solution)/shard_map/ppermute | solution.py:388
  3.0 10.5 %collective-permute-start.7 = (bf16[128,512]{1,0:T(8,128)(2,1)}, bf16[128,512]{1,0:T(8,128)(2,1)S(1)}, u32[]{:S(2)}, u32[]{:S(2)}) collective-permute-start(bf16[128,512]{1,0:T(8,128)(2,1)} %kv_ref.1), channel_id=1, source_target_pairs={{30,0},{27,1},{0,2},{29,3},{2,4},{31,5},{4,6},{1,7},{6,8},{3,9},{8... | collective-permute-start | bytes 393224 | tf_op jit(solution)/shard_map/ppermute | solution.py:388
  8.8 1.1 copy-start
  9.9 0.9 copy-start.1
  10.8 2.8 %copy-start.2 = (s32[64]{0:T(128)S(1)}, s32[64]{0:T(128)}, u32[]{:S(2)}) copy-start(s32[64]{0:T(128)} %param.19) | copy-start | bytes 772
  13.5 2.4 %collective-permute-start.8 = (bf16[256,512]{1,0:T(8,128)(2,1)S(1)}, bf16[256,512]{1,0:T(8,128)(2,1)S(1)}, u32[]{:S(2)}, u32[]{:S(2)}) collective-permute-start(bf16[256,512]{1,0:T(8,128)(2,1)S(1)} %constant_dynamic-update-slice_fusion.refs_0_), channel_id=1, source_target_pairs={{0,1},{1,0},{2,3},{3,2},{4,5},{5,4},{6,7},{7,6},{8,9},{9,8},{10,11... | collective-permute-start | bytes 786440 | tf_op jit(solution)/shard_map/ppermute | solution.py:376
  51.9 111.8 %collective-permute-start.9 = (bf16[128,1024]{1,0:T(8,128)(2,1)}, bf16[128,1024]{1,0:T(8,128)(2,1)S(1)}, u32[]{:S(2)}, u32[]{:S(2)}) collective-permute-start(bf16[128,1024]{1,0:T(8,128)(2,1)} %get-tuple-element.80), channel_id=1, source_target_pairs={{0,1},{1,0},{2,3},{3,2},{4,5},{5,4},{6,7},{7,6},{8,9},{9,8},{10,11... | collective-permute-start | bytes 786440 | tf_op jit(solution)/shard_map/ppermute | solution.py:376
  166.7 6.4 %collective-permute-start.3 = (bf16[64,1024]{1,0:T(8,128)(2,1)S(1)}, bf16[64,1024]{1,0:T(8,128)(2,1)S(1)}, u32[]{:S(2)}, u32[]{:S(2)}) collective-permute-start(bf16[64,1024]{1,0:T(8,128)(2,1)S(1)} %get-tuple-element.89), channel_id=1, source_target_pairs={{0,2},{2,0},{4,6},{6,4},{8,10},{10,8},{12,14},{14,12},{16,18},{18,... | collective-permute-start | bytes 393224 | tf_op jit(solution)/shard_map/cond/branch_1_fun/ppermute | solution.py:376
  166.8 7.6 %collective-permute-start.5 = (bf16[64,1024]{1,0:T(8,128)(2,1)S(1)}, bf16[64,1024]{1,0:T(8,128)(2,1)S(1)}, u32[]{:S(2)}, u32[]{:S(2)}) collective-permute-start(bf16[64,1024]{1,0:T(8,128)(2,1)S(1)} %get-tuple-element.90), channel_id=1, source_target_pairs={{0,6},{2,4},{4,2},{6,0},{8,14},{10,12},{12,10},{14,8},{16,22},{18,... | collective-permute-start | bytes 393224 | tf_op jit(solution)/shard_map/cond/branch_1_fun/ppermute | solution.py:376
  167.7 8.8 %collective-permute-start.4 = (bf16[64,1024]{1,0:T(8,128)(2,1)S(1)}, bf16[64,1024]{1,0:T(8,128)(2,1)S(1)}, u32[]{:S(2)}, u32[]{:S(2)}) collective-permute-start(bf16[64,1024]{1,0:T(8,128)(2,1)S(1)} %get-tuple-element.91), channel_id=1, source_target_pairs={{0,4},{2,6},{4,0},{6,2},{8,12},{10,14},{12,8},{14,10},{16,20},{18,... | collective-permute-start | bytes 393224 | tf_op jit(solution)/shard_map/cond/branch_1_fun/ppermute | solution.py:376
  177.0 0.7 copy-start.3

commit v7 on v3

--- a/solution.py
+++ b/solution.py
@@ -17,6 +17,7 @@
 VR = DH + PACK
 SAMPLE = 32
 AHEAD = 3
+SPAN = 4
 LIMIT = 1e30
 LOG2E = 1.4426950408889634
 
@@ -37,7 +38,71 @@
     ).astype(jnp.bfloat16)
 
 
-def own_kernel(q_ref, kv_ref, q3, k1o, v1o, k2o, v2o):
+GROUP = 4
+
+
+def plan_places(blocks):
+    room = blocks // 2
+    sizes = (blocks, 1, blocks, GROUP - 1, 1, blocks + (GROUP - 1) * room, GROUP * blocks)
+    return [sum(sizes[:k]) for k in range(len(sizes) + 1)]
+
+
+def make_plan(table_ref, plan_ref, blocks):
+    room = blocks // 2
+    position, here = table_ref[0], table_ref[1]
+    total = (table_ref.shape[0] - 2) // 2
+    target = 2 + total
+    place = lax.rem(position, GROUP)
+    masked, head, order, sent, small, some, whole, _ = plan_places(blocks)
+    one, zero = jnp.int32(1), jnp.int32(0)
+    for k in range(blocks):
+        block = position * blocks + k
+        outside = table_ref[2 + block] - (block * QB - W1)
+        plan_ref[masked + k] = jnp.clip(outside, 0, W1)
+    plan_ref[head] = here
+    for r in range(GROUP):
+        source = lax.bitwise_xor(place, jnp.int32(r))
+        slots = [table_ref[target + (position - place + source) * blocks + k] for k in range(blocks)]
+        far = [lax.bitwise_xor(lax.rem(lax.div(s, blocks), GROUP), source) for s in slots]
+        for k in range(blocks):
+            at = zero
+            for j in range(blocks):
+                if j != k:
+                    ahead = far[j] <= far[k] if j < k else far[j] < far[k]
+                    at = at + jnp.where(ahead, one, zero)
+            plan_ref[whole + r * blocks + at] = slots[k]
+            if r == 0:
+                plan_ref[order + k] = at
+        for distance in range(1, GROUP) if r == 0 else (r,):
+            nearer = zero
+            for k in range(blocks):
+                nearer = nearer + jnp.where(far[k] < distance, one, zero)
+            nearer = jnp.minimum(nearer, blocks - room)
+            if r == 0:
+                plan_ref[sent + distance - 1] = nearer
+            else:
+                for c in range(room):
+                    into = some + blocks + (r - 1) * room + c
+                    plan_ref[into] = plan_ref[whole + r * blocks + nearer + c]
+    for k in range(blocks):
+        plan_ref[some + k] = plan_ref[whole + k]
+
+    def most(device, so_far):
+        to = [lax.rem(lax.div(table_ref[target + device * blocks + k], blocks), GROUP) for k in range(blocks)]
+        for k in range(blocks):
+            alike = one
+            for j in range(blocks):
+                if j != k:
+                    alike = alike + jnp.where(to[j] == to[k], one, zero)
+            so_far = jnp.maximum(so_far, alike)
+        return so_far
+
+    alike = lax.fori_loop(0, total // blocks, most, zero)
+    plan_ref[small] = jnp.where(alike <= room, one, zero)
+
+
+def own_kernel(table_ref, q_ref, kv_ref, q3, k1o, v1o, k2o, v2o, plan_ref):
+    make_plan(table_ref, plan_ref, q_ref.shape[0] // QB)
     f32, bf16 = jnp.float32, jnp.bfloat16
     tokens = q_ref.shape[0]
     heads = q_ref.shape[1] // DH
@@ -55,7 +120,7 @@
         q3[pl.ds(h, tokens, stride=heads), :] = q_ref[:, h * DH : (h + 1) * DH].astype(f32)
 
 
-def attention_kernel(pairs, outputs, meta_ref, q3, k1o, v1o, k2o, v2o, w_ref, *refs):
+def attention_kernel(pairs, outputs, plan_ref, q3, k1o, v1o, k2o, v2o, w_ref, *refs):
     shards, refs = refs[:pairs], refs[pairs:]
     out_refs, refs = refs[:outputs], refs[outputs:]
     kv_ref, wbuf, wsem, k1n, k1s, v1t, v1n, k2x, v2x, rowid, laneid, part, top2, bad, rows = refs
@@ -68,6 +133,7 @@
     size = max(heads, PACK)
     pack = size // heads
     wide = min(2 * LANES, cols)
+    span = min(SPAN, QB // group)
     scale = LOG2E / np.sqrt(DH)
     f32, bf16 = jnp.float32, jnp.bfloat16
 
@@ -79,7 +145,8 @@
     weight_copy = pltpu.make_async_copy(w_ref, wbuf, wsem)
     weight_copy.start()
     blocks = tokens // QB
-    here = meta_ref[blocks]
+    masked, head, order = plan_places(blocks)[:3]
+    here = plan_ref[head]
 
     def lay(order):
         at = 0
@@ -224,13 +291,14 @@
             ]
             shift *= 2
         value = sums[0][:DH] * (1.0 / sums[0][DH : DH + 1])
-        rows[pl.ds(pl.multiple_of(g * LANES, LANES), LANES), :] = value.T
+        spot = (plan_ref[order + g * group // QB] * QB + g * group % QB) * heads
+        rows[pl.ds(pl.multiple_of(spot, LANES), LANES), :] = value.T
 
     def run(exact):
         prepare()
 
         def block(b, _):
-            inv = meta_ref[b]
+            inv = plan_ref[masked + b]
             g0 = b * (QB // group)
 
             @pl.when((b == 0) | (inv == W1))
@@ -238,26 +306,28 @@
                 reset(b * QB, inv)
 
             def fast(s, _):
-                g = g0 + s
                 work = []
-                for u in range(group):
+                for u in range(span * group):
                     work += [(u, n) for n in range(0, cols, wide)]
-                source = {u: scores(g, u) for u in range(group)}
+                at = [divmod(u, group) for u in range(span * group)]
+                first = g0 + s * span
+                source = [scores(first + k, u) for k, u in at]
                 top = total = None
                 ahead = [next(source[u]) for u, n in work[:AHEAD]]
                 for i, (u, n) in enumerate(work):
                     if i + AHEAD < len(work):
                         ahead.append(next(source[work[i + AHEAD][0]]))
                     logits = ahead.pop(0)
+                    g, v = first + at[u][0], at[u][1]
                     if n == 0:
                         top = highest(logits[:SAMPLE]) * scale
                         total = None
-                    some = mix(g, u, n, logits, top)
+                    some = mix(g, v, n, logits, top)
                     total = some if total is None else total + some
                     if n + wide == cols:
-                        keep(g, u, total, top)
-                    if i == 0:
-                        finish(jnp.maximum(g - 1, 0))
+                        keep(g, v, total, top)
+                        if v == group // 2:
+                            finish(jnp.maximum(g - 1, 0))
                 return 0
 
             def slow(s, _):
@@ -274,7 +344,7 @@
 
             if exact:
                 return lax.fori_loop(0, QB, slow, 0)
-            return lax.fori_loop(0, QB // group, fast, 0)
+            return lax.fori_loop(0, QB // group // span, fast, 0)
 
         lax.fori_loop(0, tokens // QB, block, 0)
         if exact:
@@ -302,9 +372,10 @@
 
 VMEM = pl.BlockSpec(memory_space=pltpu.VMEM)
 HBM = pl.BlockSpec(memory_space=pltpu.HBM)
-
-
-def own_layouts(queries, kv_rows):
+SMEM = pl.BlockSpec(memory_space=pltpu.SMEM)
+
+
+def own_layouts(table, queries, kv_rows):
     tokens, width = queries.shape
     heads = width // DH
     size = max(heads, PACK)
@@ -317,15 +388,16 @@
             jax.ShapeDtypeStruct((tokens // LANES, VR, LANES), bf16),
             jax.ShapeDtypeStruct((tokens * heads // size, size, DH), bf16),
             jax.ShapeDtypeStruct((tokens * heads // LANES, VR, LANES), f32),
+            jax.ShapeDtypeStruct((plan_places(tokens // QB)[-1],), jnp.int32),
         ],
-        in_specs=[VMEM] * 2,
-        out_specs=[VMEM] * 5,
+        in_specs=[SMEM] + [VMEM] * 2,
+        out_specs=[VMEM] * 5 + [SMEM],
         compiler_params=pltpu.CompilerParams(vmem_limit_bytes=16 * 2**20),
         cost_estimate=pl.CostEstimate(flops=10**9, bytes_accessed=4 * 2**20, transcendentals=0),
-    )(queries, kv_rows)
-
-
-def attended_and_projected(own, shards, meta, weight, outputs):
+    )(table, queries, kv_rows)
+
+
+def attended_and_projected(own, shards, plan, weight, outputs):
     heads = own[0].shape[0] // own[1].shape[0]
     tokens = own[1].shape[0]
     size = max(heads, PACK)
@@ -333,7 +405,7 @@
     return pl.pallas_call(
         functools.partial(attention_kernel, len(shards), outputs),
         out_shape=[jax.ShapeDtypeStruct((tokens, weight.shape[1] // outputs), f32)] * outputs,
-        in_specs=[pl.BlockSpec(memory_space=pltpu.SMEM)] + [VMEM] * 5 + [HBM] + [VMEM] * len(shards),
+        in_specs=[SMEM] + [VMEM] * 5 + [HBM] + [VMEM] * len(shards),
         out_specs=[VMEM] * outputs,
         scratch_shapes=[
             pltpu.VMEM((W1, 4 * DH), bf16),
@@ -352,11 +424,8 @@
             pltpu.VMEM((8, LANES), f32),
             pltpu.VMEM((tokens * heads, DH), f32),
         ],
-        compiler_params=pltpu.CompilerParams(vmem_limit_bytes=46 * 2**20),
-    )(meta, *own, weight, *shards)
-
-HOPS = 3
-
+        compiler_params=pltpu.CompilerParams(vmem_limit_bytes=43 * 2**20),
+    )(plan, *own, weight, *shards)
 
 def shifted(block, axis, distance):
     devices = range(lax.axis_size(axis))
@@ -374,7 +443,7 @@
     def taken(distances):
         devices = range(lax.axis_size("ctx"))
         route = [
-            ((i - d) * 2 + h, i * 2 + h) for i in devices for h, d in enumerate(distances) if i >= d
+            ((i - d) % len(devices) * 2 + h, i * 2 + h) for i in devices for h, d in enumerate(distances)
         ]
         return lax.ppermute(kv_rows, ("ctx", "head"), route)
 
@@ -383,41 +452,59 @@
     return [held, swapped(held, "head", 1)], own
 
 
+def exchanged(terms, plan, position, blocks):
+    room = blocks // 2
+    start, some_slots, whole_slots, few = plan
+
+    def added(terms):
+        return sum(terms[1:], terms[0]).astype(jnp.bfloat16)
+
+    def placed(pieces, slots):
+        tokens = blocks * QB
+        rows = (slots[:, None] * QB + np.arange(QB, dtype=np.int32)[None, :]).reshape(-1)
+        stored = position * tokens + jnp.arange(tokens, dtype=jnp.int32)
+        pick = (rows[:, None] == stored[None, :]).astype(jnp.bfloat16)
+        return lax.dot_general(
+            jnp.concatenate(pieces, axis=0),
+            pick,
+            (((0,), (0,)), ((), ())),
+            preferred_element_type=jnp.float32,
+        ).astype(jnp.bfloat16)
+
+    def some(*terms):
+        own = added(terms)
+        pieces = [own]
+        for r in range(1, GROUP):
+            rows = lax.dynamic_slice_in_dim(own, start[r - 1] * QB, room * QB, 0)
+            pieces.append(swapped(rows, "ctx", r))
+        return placed(pieces, some_slots)
+
+    def whole(*terms):
+        own = added(terms)
+        pieces = [own] + [swapped(own, "ctx", r) for r in range(1, GROUP)]
+        return placed(pieces, whole_slots)
+
+    return lax.cond(few, some, whole, *terms)
+
+
 def body(queries, kv_rows, doc_start, destination, out_weight):
-    position = lax.axis_index("ctx")
+    position = lax.axis_index("ctx").astype(jnp.int32)
     tokens = queries.shape[0]
     blocks = tokens // QB
-    group = HOPS + 1
-    back = W1 // tokens
-    shards, own = collect_window(kv_rows, back, own_layouts(queries, kv_rows))
-    first = position * blocks
-    starts = lax.dynamic_slice_in_dim(doc_start, first, blocks, 0)
-    own_rows = (first + jnp.arange(blocks, dtype=jnp.int32)) * QB
-    inval = jnp.clip(starts - (own_rows - W1), 0, W1).astype(jnp.int32)
-    place = position % group
-    slots = group * blocks
-    targets = lax.dynamic_slice_in_dim(destination, first - place * blocks, slots, 0)
-    row = jnp.arange(group * tokens, dtype=jnp.int32)
-    source = (place ^ (row // tokens)) * blocks + row % tokens // QB
-    known = source[:, None] == jnp.arange(slots, dtype=jnp.int32)[None, :]
-    target = jnp.sum(jnp.where(known, targets[None, :], 0), axis=1) * QB + row % QB
-    pick = target[:, None] == (first * QB + jnp.arange(tokens, dtype=jnp.int32))[None, :]
-    pick = pick.astype(jnp.bfloat16)
     here = lax.axis_index("head").astype(jnp.int32)
-    meta = jnp.concatenate([inval, here[None]])
+    table = jnp.concatenate([jnp.stack([position, here]), doc_start, destination])
+    own = own_layouts(table, queries, kv_rows)
+    shards, (*own, plan) = collect_window(kv_rows, W1 // tokens, own)
     outputs = 2 if len(shards) == 2 else 1
-    partials = attended_and_projected(own, shards, meta, out_weight, outputs)
+    partials = attended_and_projected(own, shards, plan, out_weight, outputs)
+    _, _, _, sent, small, some, whole, end = plan_places(blocks)
+    parts = ([plan[sent + r] for r in range(GROUP - 1)], plan[some:whole], plan[whole:end], plan[small] > 0)
+    partials, parts = lax.optimization_barrier((partials, parts))
     if outputs == 2:
-        summed = partials[1] + swapped(partials[0], "head", 1)
+        terms = [partials[1], swapped(partials[0], "head", 1)]
     else:
-        summed = lax.psum_scatter(partials[0], "head", scatter_dimension=1, tiled=True)
-    projected = summed.astype(jnp.bfloat16)
-    pieces = jnp.concatenate(
-        [projected] + [swapped(projected, "ctx", r) for r in range(1, group)], axis=0
-    )
-    return lax.dot_general(
-        pieces, pick, (((0,), (0,)), ((), ())), preferred_element_type=jnp.float32
-    ).astype(jnp.bfloat16)
+        terms = [lax.psum_scatter(partials[0], "head", scatter_dimension=1, tiled=True)]
+    return exchanged(terms, parts, position, blocks)
 
 
 def solution(mesh):

time: 186 us -> 173 us (0.930)
  starting transfers between devices: 123 us -> 115 us
  Pallas kernels: 40.8 us -> 37.7 us
  local copies, waits for them, and re-layouts: 6.42 us -> 3.59 us
  waiting for transfers between devices: 14.8 us -> 12.2 us
  loops' own time: 0 us -> 1.92 us
    ppermute x5, waiting for transfers between devices: 14.8 us -> 8.18 us  [swapped(): lax.ppermute(block, axis, [(i, i ^ bits) for i in range(lax.axis_size(axi...]
    pallas_call x1, Pallas kernels: 39.8 us -> 35.4 us  [attended_and_projected(): pl.pallas_call(functools.partial(attention_kernel, len(shards), outputs),...]
    ppermute x2, waiting for transfers between devices: 0.01 us -> 3.97 us  [taken(): return lax.ppermute(kv_rows, ('ctx', 'head'), route)]
    ppermute x2, starting transfers between devices: 8.27 us -> 4.46 us  [taken(): return lax.ppermute(kv_rows, ('ctx', 'head'), route)]
    unnamed x21 -> x9, local copies, waits for them, and re-layouts: 6.34 us -> 2.66 us
    ppermute x5, starting transfers between devices: 114 us -> 111 us  [swapped(): lax.ppermute(block, axis, [(i, i ^ bits) for i in range(lax.axis_size(axi...]
    unnamed x0 -> x1, loops' own time: none -> 1.92 us
  transfers between devices with their start and end apart: 7 -> 7, of which waited for: 4 -> 6; matrix products, arithmetic and copies ran while one was open for 0% -> 1% of each run, Pallas kernels for 1% -> 1%
where the time goes in v7:
time: 173 us
  starting transfers between devices  115 us (66%)
  Pallas kernels  37.7 us (22%)
  waiting for transfers between devices  12.2 us (7%)
  local copies, waits for them, and re-layouts  3.59 us (2%)
  loops' own time  1.92 us (1%)
    ppermute x5, starting transfers between devices, swapped(): lax.ppermute(block, axis, [(i, i ^ bits) for i in range(lax.axis_size(axi...  111 us
    pallas_call x1, Pallas kernels, attended_and_projected(): pl.pallas_call(functools.partial(attention_kernel, len(shards), outputs),...  35.4 us
    ppermute x5, waiting for transfers between devices, swapped(): lax.ppermute(block, axis, [(i, i ^ bits) for i in range(lax.axis_size(axi...  8.18 us
    ppermute x2, starting transfers between devices, taken(): return lax.ppermute(kv_rows, ('ctx', 'head'), route)  4.46 us
    ppermute x2, waiting for transfers between devices, taken(): return lax.ppermute(kv_rows, ('ctx', 'head'), route)  3.97 us
  transfers between devices with their start and end apart: 7, of which 6 were waited for; matrix products, arithmetic and copies ran while one was open for 1% of the time, Pallas kernels for 1%

profile of v7, /device:TPU:0, one launch (start us, length us, event | category | flops | bytes accessed | tf_op | source)
XLA Modules:
  0.0 172.9 jit_solution(15654343369388949927)
XLA Ops:
  0.0 3.0 %collective-permute-start.6 = (bf16[128,512]{1,0:T(8,128)(2,1)}, bf16[128,512]{1,0:T(8,128)(2,1)S(1)}, u32[]{:S(2)}, u32[]{:S(2)}) collective-permute-start(bf16[128,512]{1,0:T(8,128)(2,1)} %kv_ref.1), channel_id=1, source_target_pairs={{28,0},{25,1},{30,2},{27,3},{0,4},{29,5},{2,6},{31,7},{4,8},{1,9},... | collective-permute-start | bytes 393224 | tf_op jit(solution)/shard_map/ppermute | solution.py:448
  3.0 1.5 collective-permute-start.7
  4.5 0.7 pad_add_fusion.table_ref
  5.2 1.0 copy-done
  6.3 0.9 copy-done.1
  7.2 2.3 %shard_map.73 = (f32[2048,128]{1,0:T(8,128)S(1)}, bf16[128,128]{1,0:T(8,128)(2,1)S(1)}, bf16[1,144,128]{2,1,0:T(8,128)(2,1)S(1)}, bf16[128,16,128]{2,1,0:T(8,128...) custom-call(s32[130]{0:T(256)S(1)} %pad_add_fusion.table_ref, bf16[128,2048]{1,0:T(8,128)(2,1)S(1)} %copy-done, ...), custom_call_target="tpu_custom_call" | custom-call | flops 1000000000 | bytes 4194304 | tf_op jit(solution)/shard_map/pallas_call | solution.py:383
  9.5 0.9 collective-permute-done.6
  10.4 3.1 %collective-permute-done.7 = bf16[128,512]{1,0:T(8,128)(2,1)S(1)} collective-permute-done((bf16[128,512]{1,0:T(8,128)(2,1)}, bf16[128,512]{1,0:T(8,128)(2,1)S(1)}, u32[]{:S(2)}, u32[]{:S(2)}) %collective-permute-start.7) | collective-permute-done | bytes 131104 | tf_op jit(solution)/shard_map/ppermute | solution.py:448
  13.5 0.1 collective-permute-start.8
  13.6 0.1 slice.21
  13.6 0.1 slice.22
  13.7 0.7 fusion.24
  15.1 35.4 %shard_map.74 = (f32[128,1024]{1,0:T(8,128)S(1)}, f32[128,1024]{1,0:T(8,128)S(1)}) custom-call(s32[39]{0:T(128)S(1)} %get-tuple-element.79.plan_ref, f32[2048,128]{1,0:T(8,128)S(1)} %get-tuple-element.80.q3, bf16[128,128]{1,0:T(8,128)(2,1)S(1)} %get-tuple-element.81.k1o, bf16[1,144,128]{2,1,0:T(8,128)(2,1)S(1)} %get-tuple-element.82.v1o, ...), custom_call_target="tpu_custom_call" | custom-call | tf_op jit(solution)/shard_map/pallas_call | solution.py:405
  50.5 0.5 collective-permute-start.9
  51.0 1.5 collective-permute-done.9
  52.6 119.6 %conditional.2 = (bf16[1024,128]{1,0:T(8,128)(2,1)S(1)}) conditional(s32[]{:T(128)} %convert_element_type.16, (f32[128,1024]{1,0:T(8,128)S(1)}, f32[128,1024]{1,0:T(8,128)S(1)}, s32[16]{0:T(128)S(1)}, s32[1,32]{1,0:T(1,128)S(1)}, s32[]{:T(128)}) %tuple.27, (f32[128,1024]{1,0:T(8,128)S(1)}, f32[128,1024]{1,0:T(8,128)S(1)}, s32[]{:T(128)}, s32[]{:T(128)}, ...), branch_computations={%region_0.0_spmd, %region_1.0_spmd} | conditional | flops 138740368 | bytes 5776848
  54.6 108.8 %collective-permute-start.3 = (bf16[64,1024]{1,0:T(8,128)(2,1)S(1)}, bf16[64,1024]{1,0:T(8,128)(2,1)S(1)}, u32[]{:S(2)}, u32[]{:S(2)}) collective-permute-start(bf16[64,1024]{1,0:T(8,128)(2,1)S(1)} %get-tuple-element.97), channel_id=1, source_target_pairs={{0,2},{2,0},{4,6},{6,4},{8,10},{10,8},{12,14},{14,12},{16,18},{18,... | collective-permute-start | bytes 393224 | tf_op jit(solution)/shard_map/cond/branch_1_fun/ppermute | solution.py:436
  163.4 1.5 collective-permute-start.5
  164.9 0.1 broadcast_add_fusion.1
  165.0 0.1 add.76
  165.1 2.4 %collective-permute-done.3 = bf16[64,1024]{1,0:T(8,128)(2,1)S(1)} collective-permute-done((bf16[64,1024]{1,0:T(8,128)(2,1)S(1)}, bf16[64,1024]{1,0:T(8,128)(2,1)S(1)}, u32[]{:S(2)}, u32[]{:S(2)}) %collective-permute-start.3) | collective-permute-done | bytes 131104 | tf_op jit(solution)/shard_map/cond/branch_1_fun/ppermute | solution.py:436
  167.5 4.2 %collective-permute-done.4 = bf16[64,1024]{1,0:T(8,128)(2,1)S(1)} collective-permute-done((bf16[64,1024]{1,0:T(8,128)(2,1)S(1)}, bf16[64,1024]{1,0:T(8,128)(2,1)S(1)}, u32[]{:S(2)}, u32[]{:S(2)}) %collective-permute-start.4) | collective-permute-done | bytes 131104 | tf_op jit(solution)/shard_map/cond/branch_1_fun/ppermute | solution.py:436
  171.7 0.5 fusion.12
  172.2 0.7 copy-done.3
  (14 shorter events, 0.2 us)
Async XLA Ops:
  0.0 10.4 %collective-permute-start.6 = (bf16[128,512]{1,0:T(8,128)(2,1)}, bf16[128,512]{1,0:T(8,128)(2,1)S(1)}, u32[]{:S(2)}, u32[]{:S(2)}) collective-permute-start(bf16[128,512]{1,0:T(8,128)(2,1)} %kv_ref.1), channel_id=1, source_target_pairs={{28,0},{25,1},{30,2},{27,3},{0,4},{29,5},{2,6},{31,7},{4,8},{1,9},... | collective-permute-start | bytes 393224 | tf_op jit(solution)/shard_map/ppermute | solution.py:448
  3.0 10.5 %collective-permute-start.7 = (bf16[128,512]{1,0:T(8,128)(2,1)}, bf16[128,512]{1,0:T(8,128)(2,1)S(1)}, u32[]{:S(2)}, u32[]{:S(2)}) collective-permute-start(bf16[128,512]{1,0:T(8,128)(2,1)} %kv_ref.1), channel_id=1, source_target_pairs={{30,0},{27,1},{0,2},{29,3},{2,4},{31,5},{4,6},{1,7},{6,8},{3,9},{8... | collective-permute-start | bytes 393224 | tf_op jit(solution)/shard_map/ppermute | solution.py:448
  5.2 1.0 copy-start
  6.3 0.9 copy-start.1
  13.5 1.6 collective-permute-start.8
  15.0 37.6 %copy-start.2 = (s32[1,32]{1,0:T(1,128)S(1)}, s32[1,32]{1,0:T(1,128)}, u32[]{:S(2)}) copy-start(s32[1,32]{1,0:T(1,128)} %constant.24.clone) | copy-start | bytes 388
  50.5 2.1 %collective-permute-start.9 = (f32[128,1024]{1,0:T(8,128)S(1)}, f32[128,1024]{1,0:T(8,128)S(1)}, u32[]{:S(2)}, u32[]{:S(2)}) collective-permute-start(f32[128,1024]{1,0:T(8,128)S(1)} %get-tuple-element.91), channel_id=1, source_target_pairs={{0,1},{1,0},{2,3},{3,2},{4,5},{5,4},{6,7},{7,6},{8,9},{9,8},{10,11... | collective-permute-start | bytes 1572872 | tf_op jit(solution)/shard_map/ppermute | solution.py:436
  54.6 112.9 %collective-permute-start.3 = (bf16[64,1024]{1,0:T(8,128)(2,1)S(1)}, bf16[64,1024]{1,0:T(8,128)(2,1)S(1)}, u32[]{:S(2)}, u32[]{:S(2)}) collective-permute-start(bf16[64,1024]{1,0:T(8,128)(2,1)S(1)} %get-tuple-element.97), channel_id=1, source_target_pairs={{0,2},{2,0},{4,6},{6,4},{8,10},{10,8},{12,14},{14,12},{16,18},{18,... | collective-permute-start | bytes 393224 | tf_op jit(solution)/shard_map/cond/branch_1_fun/ppermute | solution.py:436
  163.4 8.3 %collective-permute-start.4 = (bf16[64,1024]{1,0:T(8,128)(2,1)S(1)}, bf16[64,1024]{1,0:T(8,128)(2,1)S(1)}, u32[]{:S(2)}, u32[]{:S(2)}) collective-permute-start(bf16[64,1024]{1,0:T(8,128)(2,1)S(1)} %get-tuple-element.99), channel_id=1, source_target_pairs={{0,4},{2,6},{4,0},{6,2},{8,12},{10,14},{12,8},{14,10},{16,20},{18,... | collective-permute-start | bytes 393224 | tf_op jit(solution)/shard_map/cond/branch_1_fun/ppermute | solution.py:436
  163.4 8.3 %collective-permute-start.5 = (bf16[64,1024]{1,0:T(8,128)(2,1)S(1)}, bf16[64,1024]{1,0:T(8,128)(2,1)S(1)}, u32[]{:S(2)}, u32[]{:S(2)}) collective-permute-start(bf16[64,1024]{1,0:T(8,128)(2,1)S(1)} %get-tuple-element.98), channel_id=1, source_target_pairs={{0,6},{2,4},{4,2},{6,0},{8,14},{10,12},{12,10},{14,8},{16,22},{18,... | collective-permute-start | bytes 393224 | tf_op jit(solution)/shard_map/cond/branch_1_fun/ppermute | solution.py:436
  172.2 0.7 copy-start.3
